TPU v7x, 256 devices: a whole 4x4x8 slice. The times are simulated.
256 devices in a mesh: row: 8 (over z), col: 32 (over y, x, core).
Axes of the slice: x: 4, y: 4, z: 8, core: 2. Of those that a mesh axis runs over, the one named last changes fastest.
Arguments:
- diag_block: float32 [512, 512], P(('row', 'col')), may hold values from -1 to 140, as said below
- panel: float32 [12, 8, 32, 16, 512], P(None, 'row', 'col'), may hold values from -8 to 8
- slab: float32 [12, 8, 512, 32, 256], P(None, 'row', None, 'col'), may hold values from -6 to 6
Outputs:
- diag_factor: float32 [512, 512], P(('row', 'col'))
- panel_factor: float32 [12, 8, 32, 16, 512], P(None, 'row', 'col')
- new_slab: float32 [12, 8, 512, 32, 256], P(None, 'row', None, 'col')
Inputs may be any that keep to these rules, and one draw needn't show every extreme that they name: diag_block is symmetric positive definite.
All inputs are finite; a program needn't handle non-finite values.
Results may differ from a plain program's by a relative error of at most 0.0003.
Values sent between devices are 32-bit elements; how exact they have to be, the bound alone decides.
No kernel may reach another device: no remote copies, remote signals or barrier semaphores. Data moves between devices by JAX's collectives and lax.ppermute only.
A program may use at most 128 MiB of HBM per device.

v0:
```python
import jax
import jax.numpy as jnp
import numpy as np
from jax import lax
from jax.experimental import pallas as pl
from jax.experimental.pallas import tpu as pltpu
from jax.sharding import Mesh, PartitionSpec as P

F32, BF16 = jnp.float32, jnp.bfloat16
NZ, NY, NX, NC = 8, 4, 4, 2
ALL = ("z", "y", "x", "core")
VMEM = pl.BlockSpec(memory_space=pltpu.VMEM)
HBM = pl.BlockSpec(memory_space=pl.ANY)
SMEM = pl.BlockSpec(memory_space=pltpu.SMEM)


def dot(a, b):
    return jnp.dot(a, b, precision=lax.Precision.HIGHEST, preferred_element_type=F32)


def dot_t(a, b):
    return lax.dot_general(
        a, b, (((1,), (1,)), ((), ())), precision=lax.Precision.HIGHEST, preferred_element_type=F32
    )


def row(v, j):
    return jnp.broadcast_to(v[j : j + 1, :], (8, 128))


def col(v, c):
    return jnp.broadcast_to(v[:, c : c + 1], (8, 128))


def factor_tile(read, tiles=16):
    sub = lax.broadcasted_iota(jnp.int32, (8, 128), 0)
    lane = lax.broadcasted_iota(jnp.int32, (8, 128), 1)
    left = [read(r) for r in range(tiles)]
    right = [jnp.where(lane == sub + 8 * r, 1.0, 0.0).astype(F32) for r in range(tiles)]
    up, inv = [], []
    for k in range(tiles):
        a, b = left[k], right[k]
        c = [col(a, 8 * k + j) for j in range(8)]
        ua = ub = dv = jnp.zeros((8, 128), F32)
        for j in range(8):
            at = sub == j
            piv = row(c[j], j)
            rec = 1.0 / piv
            ra, rb = row(a, j), row(b, j)
            ua, ub, dv = jnp.where(at, ra, ua), jnp.where(at, rb, ub), jnp.where(at, piv, dv)
            cj = c[j]
            for m in range(j + 1, 8):
                rm = row(c[m], j) * rec
                c[m] = jnp.where(at, rm, c[m] - cj * rm)
            ra, rb = ra * rec, rb * rec
            a, b = jnp.where(at, ra, a - cj * ra), jnp.where(at, rb, b - cj * rb)
        rs = lax.rsqrt(dv)
        up.append(jnp.where(lane >= sub + 8 * k, ua * rs, 0.0))
        inv.append(ub * rs)
        if k < tiles - 1:
            va, vb = [row(a, j) for j in range(8)], [row(b, j) for j in range(8)]
            for r in range(k + 1, tiles):
                cs = [col(left[r], 8 * k + j) for j in range(8)]

                def total(v, cs=cs):
                    p = [cs[j] * v[j] for j in range(8)]
                    return ((p[0] + p[1]) + (p[2] + p[3])) + ((p[4] + p[5]) + (p[6] + p[7]))

                left[r] = left[r] - total(va)
                right[r] = right[r] - total(vb)
    return jnp.concatenate(up, 0), jnp.concatenate(inv, 0)


def factor_step(t, w, l_ref, i_ref):
    order = w.shape[0]
    lo, hi = t * 128, (t + 1) * 128
    u, inv = factor_tile(lambda r: w[lo + 8 * r : lo + 8 * r + 8, lo:hi])
    l_ref[lo:hi, lo:hi] = u.T
    if t:
        i_ref[lo:hi, :lo] = dot(inv, i_ref[lo:hi, :lo])
    i_ref[lo:hi, lo:hi] = inv
    if hi < order:
        u12 = dot(inv, w[lo:hi, hi:])
        l21 = u12.T
        l_ref[hi:, lo:hi] = l21
        w[hi:, hi:] -= dot(l21, u12)
        i_ref[hi:, :hi] -= dot(l21, i_ref[lo:hi, :hi])


def first_kernel(where, own_ref, other_ref, w, l_ref, i_ref, tiles_ref):
    c = where[3]
    order = w.shape[0]
    per = NZ * NY * NX
    for flip, ref in enumerate((own_ref, other_ref)):
        for n in range(per):
            device = n % NZ * (NY * NX * NC) + n // NZ * NC + (c ^ flip)
            tiles_ref[pl.ds(pl.multiple_of(device * 8, 8), 8), :] = ref[n]
    for t in range(order // 128):
        w[:, t * 128 : (t + 1) * 128] = tiles_ref[pl.ds(t, order, stride=order // 128), :]
    l_ref[...] = jnp.zeros_like(l_ref)
    i_ref[...] = jnp.zeros_like(i_ref)
    factor_step(0, w, l_ref, i_ref)


def factor_first(where, own, other, order):
    shape = jax.ShapeDtypeStruct((order, order), F32)
    return pl.pallas_call(
        first_kernel,
        out_shape=(shape,) * 3,
        in_specs=[SMEM, VMEM, VMEM],
        out_specs=(VMEM,) * 3,
        scratch_shapes=[pltpu.VMEM((order * order // 128, 128), F32)],
        compiler_params=pltpu.CompilerParams(vmem_limit_bytes=16 << 20),
        cost_estimate=pl.CostEstimate(flops=6_000_000_000, bytes_accessed=3 << 20, transcendentals=0),
    )(where, own, other)


def factor_next(t, state):
    def body(w_in, l_in, i_in, w, l_ref, i_ref):
        factor_step(t, w, l_ref, i_ref)

    return pl.pallas_call(
        body,
        out_shape=tuple(jax.ShapeDtypeStruct(a.shape, F32) for a in state),
        in_specs=[VMEM] * 3,
        out_specs=(VMEM,) * 3,
        input_output_aliases={0: 0, 1: 1, 2: 2},
        compiler_params=pltpu.CompilerParams(vmem_limit_bytes=16 << 20),
        cost_estimate=pl.CostEstimate(flops=6_000_000_000, bytes_accessed=3 << 20, transcendentals=0),
    )(*state)


SLOTS = 3


def split(v):
    hi = v.astype(BF16)
    return hi, (v - hi.astype(F32)).astype(BF16)


def dot3(a, b):
    def one(p, q):
        return jnp.dot(p, q, preferred_element_type=F32)

    return one(a[0], b[0]) + (one(a[0], b[1]) + one(a[1], b[0]))


def update_kernel(where, inv, near, far, own, *refs):
    pieces, (s_ref, new_ref, mine_ref), (pb, sb, ob, win, whi, wlo, psem, ssem, osem) = refs[:-12], refs[-12:-9], refs[-9:]
    y, x, c = where[1], where[2], where[3]
    count = len(pieces)

    def slab_part(ref, i, k):
        core, off = lax.rem(c + i // 4, NC), lax.rem(i, 4)
        yy = lax.rem(y + off + core * (k - off), NY)
        xx = lax.rem(x + k + core * (off - k), NX)
        return ref.at[:, yy, xx, core]

    def loads(i, slot, do):
        for k in range(NX):
            do(pltpu.make_async_copy(slab_part(s_ref, i, k), sb.at[slot, k], ssem.at[slot, k]))

    def piece_loads(i, slot, do):
        for n in range(count):
            parts = pieces[n]

            @pl.when(i == n)
            def _(parts=parts):
                at = 0
                for j, part in enumerate(parts):
                    size = part.shape[0]
                    do(pltpu.make_async_copy(part, pb.at[slot, pl.ds(at, size)], psem.at[slot, j]))
                    at += size

    def stores(i, slot, do):
        for k in range(NX):
            do(pltpu.make_async_copy(ob.at[slot, k], slab_part(new_ref, i, k), osem.at[slot, k]))

    def start(copy):
        copy.start()

    def wait(copy):
        copy.wait()

    for i in range(SLOTS - 1):
        loads(i, i, start)
        piece_loads(i, i, start)

    part = near.shape[1]
    for n in range(NZ):
        v = near[n] if n < NZ // 2 else far[n - NZ // 2]
        bits = n % 2 * 4 + n // 2 % 2 * 2 + n // 4
        win[pl.ds(pl.multiple_of((where[0] ^ bits) * part, part), part), :] = v
    g = dot_t(win[...], inv[...])
    mine_ref[...] = dot_t(own[...], inv[...])
    w = dot(g, inv[...]).T
    whi[...], wlo[...] = split(w)

    @pl.loop(0, count)
    def _(i):
        slot = lax.rem(i, SLOTS)

        @pl.when(i + SLOTS - 1 < count)
        def _():
            later = lax.rem(i + SLOTS - 1, SLOTS)
            loads(i + SLOTS - 1, later, start)
            piece_loads(i + SLOTS - 1, later, start)

        loads(i, slot, wait)
        piece_loads(i, slot, wait)

        @pl.when(i >= SLOTS)
        def _():
            stores(i - SLOTS, slot, wait)

        got = dot3(split(pb[slot]), (whi[...], wlo[...]))
        rows = got.shape[0]
        old, new = sb.at[slot].reshape(2 * rows, 128), ob.at[slot].reshape(2 * rows, 128)
        for h in range(2):
            at = pl.ds(h, rows, stride=2)
            new[at, :] = old[at, :] - got[:, h * 128 : (h + 1) * 128]
        stores(i, slot, start)

    for i in range(count - SLOTS, count):
        stores(i, i % SLOTS, wait)


def update(where, inv, window, own, pieces, slab):
    flat = [a for parts in pieces for a in parts]
    sizes = [len(parts) for parts in pieces]
    cyc, rb, order = slab.shape[0], slab.shape[-2] // 2, inv.shape[0]
    width = slab.shape[-1] * 2

    def body(where, inv, near, far, own, *refs):
        grouped, at = [], 0
        for n in sizes:
            grouped.append(refs[at : at + n])
            at += n
        update_kernel(where, inv, near, far, own, *grouped, *refs[at:])

    return pl.pallas_call(
        body,
        out_shape=(jax.ShapeDtypeStruct(slab.shape, F32), jax.ShapeDtypeStruct(own.shape, F32)),
        in_specs=[SMEM, VMEM, VMEM, VMEM, VMEM] + [HBM] * (len(flat) + 1),
        out_specs=(HBM, VMEM),
        scratch_shapes=[
            pltpu.VMEM((SLOTS, NX * cyc * rb, order), F32),
            pltpu.VMEM((SLOTS, NX, cyc, 2 * rb, width // 2), F32),
            pltpu.VMEM((SLOTS, NX, cyc, 2 * rb, width // 2), F32),
            pltpu.VMEM((width, order), F32),
            pltpu.VMEM((order, width), BF16),
            pltpu.VMEM((order, width), BF16),
            pltpu.SemaphoreType.DMA((SLOTS, 2)),
            pltpu.SemaphoreType.DMA((SLOTS, NX)),
            pltpu.SemaphoreType.DMA((SLOTS, NX)),
        ],
        compiler_params=pltpu.CompilerParams(vmem_limit_bytes=40 << 20),
        cost_estimate=pl.CostEstimate(flops=5_000_000_000, bytes_accessed=26 << 20, transcendentals=0),
    )(where, inv, *window, own, *flat, slab)


def index(z, y, x, c):
    return ((z * NY + y) * NX + x) * NC + c


def receive(v, source):
    places = np.ndindex(NZ, NY, NX, NC)
    return lax.ppermute(v, ALL, [(index(*source(*at)), index(*at)) for at in places])


def along(phase, move):
    def source(z, y, x, c):
        return (z, y, move(x), c) if c == phase else (z, move(y), x, c)

    return source


def other_core(v):
    return receive(v, lambda z, y, x, c: (z, y, x, 1 - c))


def forward(up, down, phase):
    half = up.shape[0] // 2
    return [receive(down[:half], minus(phase)), receive(up[half:], plus(phase))]


def plus(phase):
    return along(phase, lambda i: (i + 1) % 4)


def minus(phase):
    return along(phase, lambda i: (i + 3) % 4)


def scatter(v, rows):
    core = lax.axis_index("core")
    got = other_core(v)
    sent = jnp.concatenate([jnp.where(core == 0, v[:rows], got[rows:]), jnp.where(core == 0, got[:rows], v[rows:])], 0)
    return receive(sent, lambda z, y, x, c: (y % 2 * NX + x, 2 * c + z // NX, z % NX, y // 2))


def everyone(v, axis, size):
    return lax.all_to_all(jnp.broadcast_to(v[None], (size, *v.shape)), axis, 0, 0, tiled=True)


def flip_z(b):
    return lambda z, y, x, c: (z ^ b, y, x, c)


def doubled(v, step):
    return jnp.concatenate([v, receive(v, step)], 0)


def local(diag_block, panel, slab):
    z, y, x, c = (lax.axis_index(a) for a in ALL)
    where = jnp.stack([z, y, x, c]).astype(jnp.int32)
    cyc, rb, order = panel.shape[0], panel.shape[-2], panel.shape[-1]
    p = own = panel.reshape(cyc * rb, order)
    tie = lax.optimization_barrier

    up, down = receive(p, plus(0)), receive(p, minus(0))
    d = everyone(diag_block.reshape(8, 128), "z", NZ)
    d, up, down = tie((d, up, down))
    first, second = forward(up, down, 0)
    block = jnp.concatenate([p, up, first, second, down], 0)
    up, down = receive(block, plus(1)), receive(block, minus(1))
    d = everyone(d, ("y", "x"), NY * NX).reshape(-1, 8, 128)
    w = scatter(p[: 2 * rb], rb).reshape(1, 2 * rb, order)
    other_block = other_core(block)
    d, w, other_block, up, down = tie((d, w, other_block, up, down))
    first, second = forward(up, down, 1)
    state = factor_first(where, d, other_core(d), order)
    w = doubled(w, flip_z(4))
    for t, bit in ((1, 2), (2, 1)):
        state, w = tie((state, w))
        got = receive(w, flip_z(bit))
        state = factor_next(t, state)
        if t == 1:
            w = jnp.concatenate([w, got], 0)
    state = factor_next(3, state)
    _, factor, inverse = state
    window = (w, got)
    pieces = [[block], [up], [first, second], [down]]
    pieces += [[other_block]] + [[other_core(a) for a in parts] for parts in pieces[1:]]

    view = slab.reshape(cyc, NY, NX, NC, 2 * rb, slab.shape[-1] // 2)
    new, mine = update(where, inverse, window, own, pieces, view)
    rows = diag_block.shape[0]
    own_factor = lax.dynamic_slice_in_dim(factor, index(z, y, x, c) * rows, rows, 0)
    return own_factor, mine.reshape(panel.shape), new.reshape(slab.shape)


def solution(mesh):
    fine = Mesh(np.asarray(mesh.devices).reshape(NZ, NY, NX, NC), ALL)
    placed = (
        P(ALL, None),
        P(None, "z", ("y", "x", "core"), None, None),
        P(None, "z", None, ("y", "x", "core"), None),
    )
    return jax.shard_map(local, mesh=fine, in_specs=placed, out_specs=placed, check_vma=False)
```

profile of v0, /device:TPU:1, one launch (start us, length us, event | category | flops | bytes accessed | tf_op | source)
XLA Modules:
  0.0 116.0 jit_solution(9408278206240027020)
XLA Ops:
  0.6 2.2 %collective-permute-start.1 = (f32[192,512]{1,0:T(8,128)}, f32[192,512]{1,0:T(8,128)S(1)}, u32[]{:S(2)}, u32[]{:S(2)}) collective-permute-start(f32[192,512]{1,0:T(8,128)} %bitcast.17), channel_id=1, source_target_pairs={{6,0},{25,1},{0,2},{27,3},{2,4},{29,5},{4,6},{31,7},{14,8},{1,9},{... | collective-permute-start | bytes 1179656 | tf_op jit(solution)/shard_map/ppermute | solution.py:268
  2.8 1.5 %collective-permute-start = (f32[192,512]{1,0:T(8,128)}, f32[192,512]{1,0:T(8,128)S(1)}, u32[]{:S(2)}, u32[]{:S(2)}) collective-permute-start(f32[192,512]{1,0:T(8,128)} %bitcast.18), channel_id=1, source_target_pairs={{2,0},{9,1},{4,2},{11,3},{6,4},{13,5},{0,6},{15,7},{10,8},{17,9},{... | collective-permute-start | bytes 1179656 | tf_op jit(solution)/shard_map/ppermute | solution.py:268
  4.4 0.7 broadcast_in_dim.6
  5.1 14.8 %all_to_all.10 = f32[8,8,128]{2,1,0:T(8,128)S(1)} all-to-all(f32[8,8,128]{2,1,0:T(8,128)S(1)} %broadcast_in_dim.14), channel_id=1, replica_groups=mesh['z'=8,'y'=4,'x'=4,'core'=2] {'z'}, dimensions={0} | all-to-all | bytes 65536 | tf_op jit(solution)/shard_map/all_to_all | solution.py:303
  19.9 0.0 collective-permute-done.1
  19.9 0.0 collective-permute-done
  19.9 0.1 collective-permute-start.4
  20.0 1.8 %constant_dynamic-update-slice_fusion.4 = f32[768,512]{1,0:T(8,128)} fusion(f32[192,512]{1,0:T(8,128)} %bitcast.19), kind=kLoop, calls=%fused_computation.9 | loop fusion | bytes 786432
  21.9 2.7 %collective-permute-start.5 = (f32[96,512]{1,0:T(8,128)S(1)}, f32[96,512]{1,0:T(8,128)S(1)}, u32[]{:S(2)}, u32[]{:S(2)}) collective-permute-start(f32[96,512]{1,0:T(8,128)S(1)} %slice.47), channel_id=1, source_target_pairs={{2,0},{9,1},{4,2},{11,3},{6,4},{13,5},{0,6},{15,7},{10,8},{17,9},{... | collective-permute-start | bytes 589832 | tf_op jit(solution)/shard_map/ppermute | solution.py:268
  24.6 0.8 constant_dynamic-update-slice_fusion.3
  25.4 0.0 copy-start
  25.4 0.4 collective-permute-done.4
  25.7 0.7 constant_dynamic-update-slice_fusion.2
  26.4 0.8 collective-permute-done.5
  27.2 0.7 constant_dynamic-update-slice_fusion.1
  27.9 0.8 constant_dynamic-update-slice_fusion.refs_0_
  28.7 1.2 %collective-permute-start.8 = (f32[768,512]{1,0:T(8,128)}, f32[768,512]{1,0:T(8,128)S(1)}, u32[]{:S(2)}, u32[]{:S(2)}) collective-permute-start(f32[768,512]{1,0:T(8,128)} %constant_dynamic-update-slice_fusion.refs_0_), channel_id=1, source_target_pairs={{24,0},{7,1},{26,2},{1,3},{28,4},{3,5},{30,6},{5,7},{0,8},{15,9},{... | collective-permute-start | bytes 4718600 | tf_op jit(solution)/shard_map/ppermute | solution.py:268
  29.9 1.5 %collective-permute-start.7 = (f32[768,512]{1,0:T(8,128)}, f32[768,512]{1,0:T(8,128)S(1)}, u32[]{:S(2)}, u32[]{:S(2)}) collective-permute-start(f32[768,512]{1,0:T(8,128)} %constant_dynamic-update-slice_fusion.refs_0_), channel_id=1, source_target_pairs={{8,0},{3,1},{10,2},{5,3},{12,4},{7,5},{14,6},{1,7},{16,8},{11,9},{... | collective-permute-start | bytes 4718600 | tf_op jit(solution)/shard_map/ppermute | solution.py:268
  31.4 4.2 %collective-permute-start.6 = (f32[768,512]{1,0:T(8,128)}, f32[768,512]{1,0:T(8,128)}, u32[]{:S(2)}, u32[]{:S(2)}) collective-permute-start(f32[768,512]{1,0:T(8,128)} %constant_dynamic-update-slice_fusion.refs_0_), channel_id=1, source_target_pairs={{1,0},{0,1},{3,2},{2,3},{5,4},{4,5},{7,6},{6,7},{9,8},{8,9},{11,10... | collective-permute-start | bytes 4718600 | tf_op jit(solution)/shard_map/ppermute | solution.py:268
  35.6 0.8 broadcast_in_dim.15
  36.4 6.3 %all-to-all-start.1 = ((f32[16,8,8,128]{3,2,1,0:T(8,128)}), f32[16,8,8,128]{3,2,1,0:T(8,128)}, u32[]{:S(2)}, u32[]{:S(2)}) async-start(f32[16,8,8,128]{3,2,1,0:T(8,128)} %broadcast_in_dim.15), calls=%async_computation.1 | async-start | bytes 1048576 | tf_op jit(solution)/shard_map/all_to_all | solution.py:303
  42.7 0.0 copy-done
  42.7 0.6 slice.40
  43.3 0.3 collective-permute-start.2
  43.6 1.3 %collective-permute-done.2 = f32[32,512]{1,0:T(8,128)} collective-permute-done((f32[32,512]{1,0:T(8,128)}, f32[32,512]{1,0:T(8,128)}, u32[]{:S(2)}, u32[]{:S(2)}) %collective-permute-start.2) | collective-permute-done | bytes 65568 | tf_op jit(solution)/shard_map/ppermute | solution.py:268
  44.9 0.8 slice_select_fusion.1
  45.7 5.2 %collective-permute-start.3 = (f32[32,512]{1,0:T(8,128)S(1)}, f32[32,512]{1,0:T(8,128)}, u32[]{:S(2)}, u32[]{:S(2)}) collective-permute-start(f32[32,512]{1,0:T(8,128)S(1)} %pad_maximum_fusion.2), channel_id=1, source_target_pairs={{0,0},{16,1},{32,2},{48,3},{64,4},{80,5},{96,6},{112,7},{128,8},{1... | collective-permute-start | bytes 196616 | tf_op jit(solution)/shard_map/ppermute | solution.py:268
  50.9 10.9 %collective-permute-done.3 = f32[32,512]{1,0:T(8,128)} collective-permute-done((f32[32,512]{1,0:T(8,128)S(1)}, f32[32,512]{1,0:T(8,128)}, u32[]{:S(2)}, u32[]{:S(2)}) %collective-permute-start.3) | collective-permute-done | bytes 65568 | tf_op jit(solution)/shard_map/ppermute | solution.py:268
  61.9 0.0 all-to-all-done.1
  61.9 0.0 collective-permute-done.8.refs_4_
  61.9 0.0 collective-permute-done.7.refs_1_
  61.9 0.0 collective-permute-done.6.refs_5_
  61.9 0.1 collective-permute-start.9
  62.0 0.1 collective-permute-start.10
  62.1 0.1 pad_add_fusion.where
  62.2 0.1 slice.49
  62.2 0.5 collective-permute-start.15
  62.7 0.1 slice.48
  62.8 0.2 collective-permute-start.18
  63.0 1.4 %collective-permute-start.13 = (f32[384,512]{1,0:T(8,128)S(1)}, f32[384,512]{1,0:T(8,128)S(1)}, u32[]{:S(2)}, u32[]{:S(2)}) collective-permute-start(f32[384,512]{1,0:T(8,128)S(1)} %slice.48), channel_id=1, source_target_pairs={{24,0},{7,1},{26,2},{1,3},{28,4},{3,5},{30,6},{5,7},{0,8},{15,9},{... | collective-permute-start | bytes 2359304 | tf_op jit(solution)/shard_map/ppermute | solution.py:268
  64.4 4.9 %collective-permute-done.10 = f32[1,32,512]{2,1,0:T(8,128)S(1)} collective-permute-done((f32[1,32,512]{2,1,0:T(8,128)}, f32[1,32,512]{2,1,0:T(8,128)S(1)}, u32[]{:S(2)}, u32[]{:S(2)}) %collective-permute-start.10) | collective-permute-done | bytes 65568 | tf_op jit(solution)/shard_map/ppermute | solution.py:268
  69.3 4.5 %collective-permute-start.14 = (f32[384,512]{1,0:T(8,128)S(1)}, f32[384,512]{1,0:T(8,128)S(1)}, u32[]{:S(2)}, u32[]{:S(2)}) collective-permute-start(f32[384,512]{1,0:T(8,128)S(1)} %slice.49), channel_id=1, source_target_pairs={{8,0},{3,1},{10,2},{5,3},{12,4},{7,5},{14,6},{1,7},{16,8},{11,9},{... | collective-permute-start | bytes 2359304 | tf_op jit(solution)/shard_map/ppermute | solution.py:268
  73.8 0.8 pad_maximum_fusion.1
  74.7 0.0 collective-permute-done.9.other_ref
  74.7 7.3 %shard_map.58 = (f32[512,512]{1,0:T(8,128)S(1)}, f32[512,512]{1,0:T(8,128)S(1)}, f32[512,512]{1,0:T(8,128)S(1)}) custom-call(s32[4]{0:T(128)S(1)} %pad_add_fusion.where, f32[128,8,128]{2,1,0:T(8,128)} %bitcast.5.own_ref, f32[128,8,128]{2,1,0:T(8,128)} %collective-permute-done.9.other_ref), custom_call_target="tpu_custom_call" | custom-call | flops 6000000000 | bytes 3145728 | tf_op jit(solution)/shard_map/pallas_call | solution.py:107
  82.0 0.2 collective-permute-start.11
  82.2 5.7 %shard_map.59 = (f32[512,512]{1,0:T(8,128)S(1)}, f32[512,512]{1,0:T(8,128)S(1)}, f32[512,512]{1,0:T(8,128)S(1)}) custom-call(f32[512,512]{1,0:T(8,128)S(1)} %get-tuple-element.40.w_in, f32[512,512]{1,0:T(8,128)S(1)} %get-tuple-element.41.l_in, f32[512,512]{1,0:T(8,128)S(1)} %get-tuple-element.42.i_in), custom_call_target="tpu_custom_call", output_to_operand_aliasing={{0}: (0, {}), {1}: (1, {}), {2}: (2, {})} | custom-call | flops 6000000000 | bytes 3145728 | tf_op jit(solution)/shard_map/pallas_call | solution.py:122
  87.9 2.4 %collective-permute-done.11 = f32[2,32,512]{2,1,0:T(8,128)S(1)} collective-permute-done((f32[2,32,512]{2,1,0:T(8,128)S(1)}, f32[2,32,512]{2,1,0:T(8,128)S(1)}, u32[]{:S(2)}, u32[]{:S(2)}) %collective-permute-start.11) | collective-permute-done | bytes 131104 | tf_op jit(solution)/shard_map/ppermute | solution.py:268
  90.4 0.1 collective-permute-start.12
  90.5 0.0 collective-permute-done.13.refs_2_
  90.5 0.2 collective-permute-start.16
  90.7 0.0 collective-permute-done.14.refs_3_
  90.7 0.4 collective-permute-start.17
  91.1 5.4 %shard_map.60 = (f32[512,512]{1,0:T(8,128)S(1)}, f32[512,512]{1,0:T(8,128)S(1)}, f32[512,512]{1,0:T(8,128)S(1)}) custom-call(f32[512,512]{1,0:T(8,128)S(1)} %get-tuple-element.47.w_in, f32[512,512]{1,0:T(8,128)S(1)} %get-tuple-element.48.l_in, f32[512,512]{1,0:T(8,128)S(1)} %get-tuple-element.49.i_in), custom_call_target="tpu_custom_call", output_to_operand_aliasing={{0}: (0, {}), {1}: (1, {}), {2}: (2, {})} | custom-call | flops 6000000000 | bytes 3145728 | tf_op jit(solution)/shard_map/pallas_call | solution.py:122
  96.5 5.0 %shard_map.61 = (f32[512,512]{1,0:T(8,128)S(1)}, f32[512,512]{1,0:T(8,128)S(1)}, f32[512,512]{1,0:T(8,128)S(1)}) custom-call(f32[512,512]{1,0:T(8,128)S(1)} %get-tuple-element.50.w_in, f32[512,512]{1,0:T(8,128)S(1)} %get-tuple-element.51.l_in, f32[512,512]{1,0:T(8,128)S(1)} %get-tuple-element.52.i_in), custom_call_target="tpu_custom_call", output_to_operand_aliasing={{0}: (0, {}), {1}: (1, {}), {2}: (2, {})} | custom-call | flops 6000000000 | bytes 3145728 | tf_op jit(solution)/shard_map/pallas_call | solution.py:122
  101.5 0.6 constant_dynamic-slice_fusion
  102.1 0.0 collective-permute-done.12.far
  102.1 0.0 collective-permute-done.16.refs_7_
  102.1 0.0 collective-permute-done.17.refs_8_
  102.1 0.0 collective-permute-done.15.refs_6_
  102.1 0.0 collective-permute-done.18.refs_9_
  102.1 13.6 %shard_map.62 = (f32[12,4,4,2,32,128]{5,4,3,2,1,0:T(8,128)}, f32[192,512]{1,0:T(8,128)}) custom-call(s32[4]{0:T(128)S(1)} %pad_add_fusion.where, f32[512,512]{1,0:T(8,128)S(1)} %get-tuple-element.54.inv, f32[4,32,512]{2,1,0:T(8,128)S(1)} %pad_maximum_fusion.near, f32[4,32,512]{2,1,0:T(8,128)S(1)} %collective-permute-done.12.far, f32[192,512]{1,0:T(8,128)S(1)} %bitcast.20, ...), custom_call_target="tpu_custom_call" | custom-call | flops 5000000000 | bytes 27262976 | tf_op jit(solution)/shard_map/pallas_call | solution.py:241
  (5 shorter events, 0.1 us)
Async XLA Ops:
  0.6 19.3 %collective-permute-start.1 = (f32[192,512]{1,0:T(8,128)}, f32[192,512]{1,0:T(8,128)S(1)}, u32[]{:S(2)}, u32[]{:S(2)}) collective-permute-start(f32[192,512]{1,0:T(8,128)} %bitcast.17), channel_id=1, source_target_pairs={{6,0},{25,1},{0,2},{27,3},{2,4},{29,5},{4,6},{31,7},{14,8},{1,9},{... | collective-permute-start | bytes 1179656 | tf_op jit(solution)/shard_map/ppermute | solution.py:268
  2.8 17.1 %collective-permute-start = (f32[192,512]{1,0:T(8,128)}, f32[192,512]{1,0:T(8,128)S(1)}, u32[]{:S(2)}, u32[]{:S(2)}) collective-permute-start(f32[192,512]{1,0:T(8,128)} %bitcast.18), channel_id=1, source_target_pairs={{2,0},{9,1},{4,2},{11,3},{6,4},{13,5},{0,6},{15,7},{10,8},{17,9},{... | collective-permute-start | bytes 1179656 | tf_op jit(solution)/shard_map/ppermute | solution.py:268
  19.9 5.8 %collective-permute-start.4 = (f32[96,512]{1,0:T(8,128)S(1)}, f32[96,512]{1,0:T(8,128)S(1)}, u32[]{:S(2)}, u32[]{:S(2)}) collective-permute-start(f32[96,512]{1,0:T(8,128)S(1)} %slice.46), channel_id=1, source_target_pairs={{6,0},{25,1},{0,2},{27,3},{2,4},{29,5},{4,6},{31,7},{14,8},{1,9},{... | collective-permute-start | bytes 589832 | tf_op jit(solution)/shard_map/ppermute | solution.py:268
  21.9 5.4 %collective-permute-start.5 = (f32[96,512]{1,0:T(8,128)S(1)}, f32[96,512]{1,0:T(8,128)S(1)}, u32[]{:S(2)}, u32[]{:S(2)}) collective-permute-start(f32[96,512]{1,0:T(8,128)S(1)} %slice.47), channel_id=1, source_target_pairs={{2,0},{9,1},{4,2},{11,3},{6,4},{13,5},{0,6},{15,7},{10,8},{17,9},{... | collective-permute-start | bytes 589832 | tf_op jit(solution)/shard_map/ppermute | solution.py:268
  25.4 17.3 %copy-start = (f32[12,1,1,16,512]{4,3,2,1,0:T(8,128)S(1)}, f32[12,1,1,16,512]{4,3,2,1,0:T(8,128)}, u32[]{:S(2)}) copy-start(f32[12,1,1,16,512]{4,3,2,1,0:T(8,128)} %param.4) | copy-start | bytes 1179652
  28.7 33.2 %collective-permute-start.8 = (f32[768,512]{1,0:T(8,128)}, f32[768,512]{1,0:T(8,128)S(1)}, u32[]{:S(2)}, u32[]{:S(2)}) collective-permute-start(f32[768,512]{1,0:T(8,128)} %constant_dynamic-update-slice_fusion.refs_0_), channel_id=1, source_target_pairs={{24,0},{7,1},{26,2},{1,3},{28,4},{3,5},{30,6},{5,7},{0,8},{15,9},{... | collective-permute-start | bytes 4718600 | tf_op jit(solution)/shard_map/ppermute | solution.py:268
  29.9 32.0 %collective-permute-start.7 = (f32[768,512]{1,0:T(8,128)}, f32[768,512]{1,0:T(8,128)S(1)}, u32[]{:S(2)}, u32[]{:S(2)}) collective-permute-start(f32[768,512]{1,0:T(8,128)} %constant_dynamic-update-slice_fusion.refs_0_), channel_id=1, source_target_pairs={{8,0},{3,1},{10,2},{5,3},{12,4},{7,5},{14,6},{1,7},{16,8},{11,9},{... | collective-permute-start | bytes 4718600 | tf_op jit(solution)/shard_map/ppermute | solution.py:268
  31.4 30.5 %collective-permute-start.6 = (f32[768,512]{1,0:T(8,128)}, f32[768,512]{1,0:T(8,128)}, u32[]{:S(2)}, u32[]{:S(2)}) collective-permute-start(f32[768,512]{1,0:T(8,128)} %constant_dynamic-update-slice_fusion.refs_0_), channel_id=1, source_target_pairs={{1,0},{0,1},{3,2},{2,3},{5,4},{4,5},{7,6},{6,7},{9,8},{8,9},{11,10... | collective-permute-start | bytes 4718600 | tf_op jit(solution)/shard_map/ppermute | solution.py:268
  36.4 25.4 %all-to-all-start.1 = ((f32[16,8,8,128]{3,2,1,0:T(8,128)}), f32[16,8,8,128]{3,2,1,0:T(8,128)}, u32[]{:S(2)}, u32[]{:S(2)}) async-start(f32[16,8,8,128]{3,2,1,0:T(8,128)} %broadcast_in_dim.15), calls=%async_computation.1 | async-start | bytes 1048576 | tf_op jit(solution)/shard_map/all_to_all | solution.py:303
  43.3 1.6 %collective-permute-start.2 = (f32[32,512]{1,0:T(8,128)}, f32[32,512]{1,0:T(8,128)}, u32[]{:S(2)}, u32[]{:S(2)}) collective-permute-start(f32[32,512]{1,0:T(8,128)} %bitcast.7), channel_id=1, source_target_pairs={{1,0},{0,1},{3,2},{2,3},{5,4},{4,5},{7,6},{6,7},{9,8},{8,9},{11,10... | collective-permute-start | bytes 196616 | tf_op jit(solution)/shard_map/ppermute | solution.py:268
  45.7 16.1 %collective-permute-start.3 = (f32[32,512]{1,0:T(8,128)S(1)}, f32[32,512]{1,0:T(8,128)}, u32[]{:S(2)}, u32[]{:S(2)}) collective-permute-start(f32[32,512]{1,0:T(8,128)S(1)} %pad_maximum_fusion.2), channel_id=1, source_target_pairs={{0,0},{16,1},{32,2},{48,3},{64,4},{80,5},{96,6},{112,7},{128,8},{1... | collective-permute-start | bytes 196616 | tf_op jit(solution)/shard_map/ppermute | solution.py:268
  61.9 12.8 %collective-permute-start.9 = (f32[128,8,128]{2,1,0:T(8,128)}, f32[128,8,128]{2,1,0:T(8,128)}, u32[]{:S(2)}, u32[]{:S(2)}) collective-permute-start(f32[128,8,128]{2,1,0:T(8,128)} %bitcast.5.own_ref), channel_id=1, source_target_pairs={{1,0},{0,1},{3,2},{2,3},{5,4},{4,5},{7,6},{6,7},{9,8},{8,9},{11,10... | collective-permute-start | bytes 1572872 | tf_op jit(solution)/shard_map/ppermute | solution.py:268
  62.0 7.3 %collective-permute-start.10 = (f32[1,32,512]{2,1,0:T(8,128)}, f32[1,32,512]{2,1,0:T(8,128)S(1)}, u32[]{:S(2)}, u32[]{:S(2)}) collective-permute-start(f32[1,32,512]{2,1,0:T(8,128)} %bitcast.9), channel_id=1, source_target_pairs={{128,0},{129,1},{130,2},{131,3},{132,4},{133,5},{134,6},{135,7},{1... | collective-permute-start | bytes 196616 | tf_op jit(solution)/shard_map/ppermute | solution.py:268
  62.2 39.9 %collective-permute-start.15 = (f32[768,512]{1,0:T(8,128)S(1)}, f32[768,512]{1,0:T(8,128)S(1)}, u32[]{:S(2)}, u32[]{:S(2)}) collective-permute-start(f32[768,512]{1,0:T(8,128)S(1)} %collective-permute-done.7.refs_1_), channel_id=1, source_target_pairs={{1,0},{0,1},{3,2},{2,3},{5,4},{4,5},{7,6},{6,7},{9,8},{8,9},{11,10... | collective-permute-start | bytes 4718600 | tf_op jit(solution)/shard_map/ppermute | solution.py:268
  62.8 39.4 %collective-permute-start.18 = (f32[768,512]{1,0:T(8,128)S(1)}, f32[768,512]{1,0:T(8,128)S(1)}, u32[]{:S(2)}, u32[]{:S(2)}) collective-permute-start(f32[768,512]{1,0:T(8,128)S(1)} %collective-permute-done.8.refs_4_), channel_id=1, source_target_pairs={{1,0},{0,1},{3,2},{2,3},{5,4},{4,5},{7,6},{6,7},{9,8},{8,9},{11,10... | collective-permute-start | bytes 4718600 | tf_op jit(solution)/shard_map/ppermute | solution.py:268
  63.0 27.5 %collective-permute-start.13 = (f32[384,512]{1,0:T(8,128)S(1)}, f32[384,512]{1,0:T(8,128)S(1)}, u32[]{:S(2)}, u32[]{:S(2)}) collective-permute-start(f32[384,512]{1,0:T(8,128)S(1)} %slice.48), channel_id=1, source_target_pairs={{24,0},{7,1},{26,2},{1,3},{28,4},{3,5},{30,6},{5,7},{0,8},{15,9},{... | collective-permute-start | bytes 2359304 | tf_op jit(solution)/shard_map/ppermute | solution.py:268
  69.3 21.4 %collective-permute-start.14 = (f32[384,512]{1,0:T(8,128)S(1)}, f32[384,512]{1,0:T(8,128)S(1)}, u32[]{:S(2)}, u32[]{:S(2)}) collective-permute-start(f32[384,512]{1,0:T(8,128)S(1)} %slice.49), channel_id=1, source_target_pairs={{8,0},{3,1},{10,2},{5,3},{12,4},{7,5},{14,6},{1,7},{16,8},{11,9},{... | collective-permute-start | bytes 2359304 | tf_op jit(solution)/shard_map/ppermute | solution.py:268
  82.0 8.4 %collective-permute-start.11 = (f32[2,32,512]{2,1,0:T(8,128)S(1)}, f32[2,32,512]{2,1,0:T(8,128)S(1)}, u32[]{:S(2)}, u32[]{:S(2)}) collective-permute-start(f32[2,32,512]{2,1,0:T(8,128)S(1)} %pad_maximum_fusion.1), channel_id=1, source_target_pairs={{64,0},{65,1},{66,2},{67,3},{68,4},{69,5},{70,6},{71,7},{72,8},{73... | collective-permute-start | bytes 393224 | tf_op jit(solution)/shard_map/ppermute | solution.py:268
  90.4 11.7 %collective-permute-start.12 = (f32[4,32,512]{2,1,0:T(8,128)S(1)}, f32[4,32,512]{2,1,0:T(8,128)S(1)}, u32[]{:S(2)}, u32[]{:S(2)}) collective-permute-start(f32[4,32,512]{2,1,0:T(8,128)S(1)} %pad_maximum_fusion.near), channel_id=1, source_target_pairs={{32,0},{33,1},{34,2},{35,3},{36,4},{37,5},{38,6},{39,7},{40,8},{41... | collective-permute-start | bytes 786440 | tf_op jit(solution)/shard_map/ppermute | solution.py:268
  90.5 11.6 %collective-permute-start.16 = (f32[384,512]{1,0:T(8,128)S(1)}, f32[384,512]{1,0:T(8,128)S(1)}, u32[]{:S(2)}, u32[]{:S(2)}) collective-permute-start(f32[384,512]{1,0:T(8,128)S(1)} %collective-permute-done.13.refs_2_), channel_id=1, source_target_pairs={{1,0},{0,1},{3,2},{2,3},{5,4},{4,5},{7,6},{6,7},{9,8},{8,9},{11,10... | collective-permute-start | bytes 2359304 | tf_op jit(solution)/shard_map/ppermute | solution.py:268
  90.7 11.4 %collective-permute-start.17 = (f32[384,512]{1,0:T(8,128)S(1)}, f32[384,512]{1,0:T(8,128)S(1)}, u32[]{:S(2)}, u32[]{:S(2)}) collective-permute-start(f32[384,512]{1,0:T(8,128)S(1)} %collective-permute-done.14.refs_3_), channel_id=1, source_target_pairs={{1,0},{0,1},{3,2},{2,3},{5,4},{4,5},{7,6},{6,7},{9,8},{8,9},{11,10... | collective-permute-start | bytes 2359304 | tf_op jit(solution)/shard_map/ppermute | solution.py:268
where the time goes:
time: 116 us
  Pallas kernels  37 us (32%)
  starting transfers between devices  32.9 us (28%)
  waiting for transfers between devices  20.8 us (18%)
  blocking collectives  14.8 us (13%)
  local copies, waits for them, and re-layouts  7.67 us (7%)
  other arithmetic  1.74 us (2%)
    ppermute x19, starting transfers between devices, receive(): lax.ppermute(v, ALL, [(index(*source(*at)), index(*at)) for at in places])  26.6 us
    ppermute x19, waiting for transfers between devices, receive(): lax.ppermute(v, ALL, [(index(*source(*at)), index(*at)) for at in places])  20.8 us
    pallas_call x3, Pallas kernels, factor_next(): pl.pallas_call(body, out_shape=tuple((jax.ShapeDtypeStruct(a.shape, F32)...  16.1 us
    all_to_all x1, blocking collectives, everyone(): lax.all_to_all(jnp.broadcast_to(v[None], (size, *v.shape)), axis, 0, 0, t...  14.8 us
    pallas_call x1, Pallas kernels, update(): pl.pallas_call(body, out_shape=(jax.ShapeDtypeStruct(slab.shape, F32), ja...  13.6 us
    pallas_call x1, Pallas kernels, factor_first(): pl.pallas_call(first_kernel, out_shape=(shape,) * 3, in_specs=[SMEM, VMEM...  7.27 us
    all_to_all x1, starting transfers between devices, everyone(): lax.all_to_all(jnp.broadcast_to(v[None], (size, *v.shape)), axis, 0, 0, t...  6.26 us
    unnamed x6, local copies, waits for them, and re-layouts  3.97 us
  transfers between devices with their start and end apart: 20, of which 6 were waited for; matrix products, arithmetic and copies ran while one was open for 7% of the time, Pallas kernels for 20%

commit v1 on v0

--- a/solution.py
+++ b/solution.py
@@ -323,25 +323,25 @@
     d, up, down = tie((d, up, down))
     first, second = forward(up, down, 0)
     block = jnp.concatenate([p, up, first, second, down], 0)
-    up, down = receive(block, plus(1)), receive(block, minus(1))
     d = everyone(d, ("y", "x"), NY * NX).reshape(-1, 8, 128)
     w = scatter(p[: 2 * rb], rb).reshape(1, 2 * rb, order)
-    other_block = other_core(block)
-    d, w, other_block, up, down = tie((d, w, other_block, up, down))
-    first, second = forward(up, down, 1)
+    d, block = tie((d, block))
+    up, down = receive(block, plus(1)), receive(block, minus(1))
     state = factor_first(where, d, other_core(d), order)
-    w = doubled(w, flip_z(4))
-    for t, bit in ((1, 2), (2, 1)):
-        state, w = tie((state, w))
+    for t, bit in ((1, 4), (2, 2), (3, 1)):
+        if t == 2:
+            state, w, up, down = tie((state, w, up, down))
+            first, second = forward(up, down, 1)
+        else:
+            state, w = tie((state, w))
         got = receive(w, flip_z(bit))
         state = factor_next(t, state)
-        if t == 1:
+        if bit > 1:
             w = jnp.concatenate([w, got], 0)
-    state = factor_next(3, state)
     _, factor, inverse = state
     window = (w, got)
     pieces = [[block], [up], [first, second], [down]]
-    pieces += [[other_block]] + [[other_core(a) for a in parts] for parts in pieces[1:]]
+    pieces += [[other_core(a) for a in parts] for parts in pieces]
 
     view = slab.reshape(cyc, NY, NX, NC, 2 * rb, slab.shape[-1] // 2)
     new, mine = update(where, inverse, window, own, pieces, view)

time: 116 us -> 112 us (0.966)
  starting transfers between devices: 32.9 us -> 25.3 us
  local copies, waits for them, and re-layouts: 7.67 us -> 14.9 us
  waiting for transfers between devices: 20.8 us -> 17.2 us
    ppermute x19, starting transfers between devices: 26.6 us -> 18.8 us  [receive(): lax.ppermute(v, ALL, [(index(*source(*at)), index(*at)) for at in places])]
    unnamed x6 -> x30, local copies, waits for them, and re-layouts: 3.97 us -> 9.49 us
    ppermute x19, waiting for transfers between devices: 20.8 us -> 17.2 us  [receive(): lax.ppermute(v, ALL, [(index(*source(*at)), index(*at)) for at in places])]
    slice x4, local copies, waits for them, and re-layouts: 0.13 us -> 1.88 us  [forward(): return [receive(down[:half], minus(phase)), receive(up[half:], plus(phase))]]
  transfers between devices with their start and end apart: 20 -> 20, of which waited for: 6 -> 5; matrix products, arithmetic and copies ran while one was open for 7% -> 8% of each run, Pallas kernels for 20% -> 21%
where the time goes in v1:
time: 112 us; the launch traced here: 111 us
  Pallas kernels  36.9 us (33%)
  starting transfers between devices  25.3 us (23%)
  waiting for transfers between devices  17.2 us (15%)
  local copies, waits for them, and re-layouts  14.9 us (13%)
  blocking collectives  14.8 us (13%)
    ppermute x19, starting transfers between devices, receive(): lax.ppermute(v, ALL, [(index(*source(*at)), index(*at)) for at in places])  18.8 us
    ppermute x19, waiting for transfers between devices, receive(): lax.ppermute(v, ALL, [(index(*source(*at)), index(*at)) for at in places])  17.2 us
    pallas_call x3, Pallas kernels, factor_next(): pl.pallas_call(body, out_shape=tuple((jax.ShapeDtypeStruct(a.shape, F32)...  16.1 us
    all_to_all x1, blocking collectives, everyone(): lax.all_to_all(jnp.broadcast_to(v[None], (size, *v.shape)), axis, 0, 0, t...  14.8 us
    pallas_call x1, Pallas kernels, update(): pl.pallas_call(body, out_shape=(jax.ShapeDtypeStruct(slab.shape, F32), ja...  13.6 us
    unnamed x30, local copies, waits for them, and re-layouts  9.49 us
    pallas_call x1, Pallas kernels, factor_first(): pl.pallas_call(first_kernel, out_shape=(shape,) * 3, in_specs=[SMEM, VMEM...  7.28 us
    all_to_all x1, starting transfers between devices, everyone(): lax.all_to_all(jnp.broadcast_to(v[None], (size, *v.shape)), axis, 0, 0, t...  6.51 us
  transfers between devices with their start and end apart: 20, of which 5 were waited for; matrix products, arithmetic and copies ran while one was open for 8% of the time, Pallas kernels for 21%

profile of v1, /device:TPU:1, one launch (start us, length us, event | category | flops | bytes accessed | tf_op | source)
XLA Modules:
  0.0 111.2 jit_solution(15864741213337975835)
XLA Ops:
  0.6 2.2 %collective-permute-start.1 = (f32[192,512]{1,0:T(8,128)}, f32[192,512]{1,0:T(8,128)S(1)}, u32[]{:S(2)}, u32[]{:S(2)}) collective-permute-start(f32[192,512]{1,0:T(8,128)} %bitcast.17), channel_id=1, source_target_pairs={{6,0},{25,1},{0,2},{27,3},{2,4},{29,5},{4,6},{31,7},{14,8},{1,9},{... | collective-permute-start | bytes 1179656 | tf_op jit(solution)/shard_map/ppermute | solution.py:268
  2.8 1.5 %collective-permute-start = (f32[192,512]{1,0:T(8,128)}, f32[192,512]{1,0:T(8,128)S(1)}, u32[]{:S(2)}, u32[]{:S(2)}) collective-permute-start(f32[192,512]{1,0:T(8,128)} %bitcast.18), channel_id=1, source_target_pairs={{2,0},{9,1},{4,2},{11,3},{6,4},{13,5},{0,6},{15,7},{10,8},{17,9},{... | collective-permute-start | bytes 1179656 | tf_op jit(solution)/shard_map/ppermute | solution.py:268
  4.4 0.7 broadcast_in_dim.6
  5.1 14.8 %all_to_all.10 = f32[8,8,128]{2,1,0:T(8,128)S(1)} all-to-all(f32[8,8,128]{2,1,0:T(8,128)S(1)} %broadcast_in_dim.14), channel_id=1, replica_groups=mesh['z'=8,'y'=4,'x'=4,'core'=2] {'z'}, dimensions={0} | all-to-all | bytes 65536 | tf_op jit(solution)/shard_map/all_to_all | solution.py:303
  19.9 0.0 collective-permute-done.1
  19.9 0.0 collective-permute-done
  19.9 0.1 collective-permute-start.2
  20.0 0.8 broadcast_in_dim.15
  20.9 6.5 %all-to-all-start.1 = ((f32[16,8,8,128]{3,2,1,0:T(8,128)}), f32[16,8,8,128]{3,2,1,0:T(8,128)}, u32[]{:S(2)}, u32[]{:S(2)}) async-start(f32[16,8,8,128]{3,2,1,0:T(8,128)} %broadcast_in_dim.15), calls=%async_computation.1 | async-start | bytes 1048576 | tf_op jit(solution)/shard_map/all_to_all | solution.py:303
  27.4 0.8 constant_dynamic-update-slice_fusion.4
  28.2 2.6 %collective-permute-start.3 = (f32[96,512]{1,0:T(8,128)S(1)}, f32[96,512]{1,0:T(8,128)S(1)}, u32[]{:S(2)}, u32[]{:S(2)}) collective-permute-start(f32[96,512]{1,0:T(8,128)S(1)} %slice.39), channel_id=1, source_target_pairs={{2,0},{9,1},{4,2},{11,3},{6,4},{13,5},{0,6},{15,7},{10,8},{17,9},{... | collective-permute-start | bytes 589832 | tf_op jit(solution)/shard_map/ppermute | solution.py:268
  30.8 0.8 constant_dynamic-update-slice_fusion.3
  31.6 0.0 collective-permute-done.2
  31.6 0.7 constant_dynamic-update-slice_fusion.2
  32.3 5.7 %collective-permute-done.3 = f32[96,512]{1,0:T(8,128)S(1)} collective-permute-done((f32[96,512]{1,0:T(8,128)S(1)}, f32[96,512]{1,0:T(8,128)S(1)}, u32[]{:S(2)}, u32[]{:S(2)}) %collective-permute-start.3) | collective-permute-done | bytes 196640 | tf_op jit(solution)/shard_map/ppermute | solution.py:268
  38.0 0.7 constant_dynamic-update-slice_fusion.1
  38.7 0.8 constant_dynamic-update-slice_fusion.refs_0_
  39.5 0.0 all-to-all-done.1
  39.5 1.4 %collective-permute-start.4 = (f32[128,8,128]{2,1,0:T(8,128)}, f32[128,8,128]{2,1,0:T(8,128)}, u32[]{:S(2)}, u32[]{:S(2)}) collective-permute-start(f32[128,8,128]{2,1,0:T(8,128)} %bitcast.5.own_ref), channel_id=1, source_target_pairs={{1,0},{0,1},{3,2},{2,3},{5,4},{4,5},{7,6},{6,7},{9,8},{8,9},{11,10... | collective-permute-start | bytes 1572872 | tf_op jit(solution)/shard_map/ppermute | solution.py:268
  40.9 0.6 slice.42
  41.5 0.0 collective-permute-start.5
  41.5 0.1 pad_add_fusion.where
  41.6 1.0 collective-permute-start.9
  42.6 1.7 %collective-permute-start.8 = (f32[768,512]{1,0:T(8,128)}, f32[768,512]{1,0:T(8,128)S(1)}, u32[]{:S(2)}, u32[]{:S(2)}) collective-permute-start(f32[768,512]{1,0:T(8,128)} %constant_dynamic-update-slice_fusion.refs_0_), channel_id=1, source_target_pairs={{8,0},{3,1},{10,2},{5,3},{12,4},{7,5},{14,6},{1,7},{16,8},{11,9},{... | collective-permute-start | bytes 4718600 | tf_op jit(solution)/shard_map/ppermute | solution.py:268
  44.3 0.0 collective-permute-done.5
  44.3 0.8 slice_select_fusion.1
  45.1 4.2 %collective-permute-start.6 = (f32[32,512]{1,0:T(8,128)S(1)}, f32[32,512]{1,0:T(8,128)S(1)}, u32[]{:S(2)}, u32[]{:S(2)}) collective-permute-start(f32[32,512]{1,0:T(8,128)S(1)} %pad_maximum_fusion.2), channel_id=1, source_target_pairs={{0,0},{16,1},{32,2},{48,3},{64,4},{80,5},{96,6},{112,7},{128,8},{1... | collective-permute-start | bytes 196616 | tf_op jit(solution)/shard_map/ppermute | solution.py:268
  49.3 0.1 collective-permute-start.14
  49.4 0.0 collective-permute-done.4.other_ref
  49.4 7.3 %shard_map.58 = (f32[512,512]{1,0:T(8,128)S(1)}, f32[512,512]{1,0:T(8,128)S(1)}, f32[512,512]{1,0:T(8,128)S(1)}) custom-call(s32[4]{0:T(128)S(1)} %pad_add_fusion.where, f32[128,8,128]{2,1,0:T(8,128)} %bitcast.5.own_ref, f32[128,8,128]{2,1,0:T(8,128)} %collective-permute-done.4.other_ref), custom_call_target="tpu_custom_call" | custom-call | flops 6000000000 | bytes 3145728 | tf_op jit(solution)/shard_map/pallas_call | solution.py:107
  56.7 8.7 %collective-permute-done.6 = f32[32,512]{1,0:T(8,128)S(1)} collective-permute-done((f32[32,512]{1,0:T(8,128)S(1)}, f32[32,512]{1,0:T(8,128)S(1)}, u32[]{:S(2)}, u32[]{:S(2)}) %collective-permute-start.6) | collective-permute-done | bytes 65568 | tf_op jit(solution)/shard_map/ppermute | solution.py:268
  65.5 0.0 collective-permute-start.7
  65.5 5.7 %shard_map.59 = (f32[512,512]{1,0:T(8,128)S(1)}, f32[512,512]{1,0:T(8,128)S(1)}, f32[512,512]{1,0:T(8,128)S(1)}) custom-call(f32[512,512]{1,0:T(8,128)S(1)} %get-tuple-element.42.w_in, f32[512,512]{1,0:T(8,128)S(1)} %get-tuple-element.43.l_in, f32[512,512]{1,0:T(8,128)S(1)} %get-tuple-element.44.i_in), custom_call_target="tpu_custom_call", output_to_operand_aliasing={{0}: (0, {}), {1}: (1, {}), {2}: (2, {})} | custom-call | flops 6000000000 | bytes 3145728 | tf_op jit(solution)/shard_map/pallas_call | solution.py:122
  71.2 0.0 copy-start.7
  71.2 1.3 %collective-permute-done.7 = f32[1,32,512]{2,1,0:T(8,128)S(1)} collective-permute-done((f32[1,32,512]{2,1,0:T(8,128)S(1)}, f32[1,32,512]{2,1,0:T(8,128)S(1)}, u32[]{:S(2)}, u32[]{:S(2)}) %collective-permute-start.7) | collective-permute-done | bytes 65568 | tf_op jit(solution)/shard_map/ppermute | solution.py:268
  72.5 0.0 collective-permute-done.9.refs_4_
  72.5 0.0 collective-permute-done.8.refs_1_
  72.5 0.1 collective-permute-start.10
  72.6 0.9 slice.48
  73.6 0.0 collective-permute-start.12
  73.6 0.9 slice.49
  74.5 2.8 %collective-permute-start.13 = (f32[384,512]{1,0:T(8,128)}, f32[384,512]{1,0:T(8,128)}, u32[]{:S(2)}, u32[]{:S(2)}) collective-permute-start(f32[384,512]{1,0:T(8,128)} %slice.49), channel_id=1, source_target_pairs={{8,0},{3,1},{10,2},{5,3},{12,4},{7,5},{14,6},{1,7},{16,8},{11,9},{... | collective-permute-start | bytes 2359304 | tf_op jit(solution)/shard_map/ppermute | solution.py:268
  77.2 0.0 collective-permute-start.15
  77.3 0.6 collective-permute-done.10
  77.9 0.7 copy-done.11
  78.5 1.2 %copy-done.2 = f32[512,512]{1,0:T(8,128)S(1)} copy-done((f32[512,512]{1,0:T(8,128)S(1)}, f32[512,512]{1,0:T(8,128)}, u32[]{:S(2)}) %copy-start.2) | copy-done | bytes 1048600
  79.8 1.2 %copy-done.6 = f32[512,512]{1,0:T(8,128)S(1)} copy-done((f32[512,512]{1,0:T(8,128)S(1)}, f32[512,512]{1,0:T(8,128)}, u32[]{:S(2)}) %copy-start.6) | copy-done | bytes 1048600
  81.0 1.2 %copy-done.8 = f32[512,512]{1,0:T(8,128)S(1)} copy-done((f32[512,512]{1,0:T(8,128)S(1)}, f32[512,512]{1,0:T(8,128)}, u32[]{:S(2)}) %copy-start.8) | copy-done | bytes 1048600
  82.2 5.4 %shard_map.60 = (f32[512,512]{1,0:T(8,128)S(1)}, f32[512,512]{1,0:T(8,128)S(1)}, f32[512,512]{1,0:T(8,128)S(1)}) custom-call(f32[512,512]{1,0:T(8,128)S(1)} %copy-done.8, f32[512,512]{1,0:T(8,128)S(1)} %copy-done.6, f32[512,512]{1,0:T(8,128)S(1)} %copy-done.2), custom_call_target="tpu_custom_call", output_to_operand_aliasing={{0}: (0, {}), {1}: (1, {}), {2}: (2, {})} | custom-call | flops 6000000000 | bytes 3145728 | tf_op jit(solution)/shard_map/pallas_call | solution.py:122
  87.6 0.0 collective-permute-done.12.refs_2_
  87.6 0.6 collective-permute-start.16
  88.2 0.1 collective-permute-start.17
  88.4 0.0 collective-permute-done.14.refs_5_
  88.4 0.4 collective-permute-start.11
  88.8 5.0 %shard_map.61 = (f32[512,512]{1,0:T(8,128)S(1)}, f32[512,512]{1,0:T(8,128)S(1)}, f32[512,512]{1,0:T(8,128)S(1)}) custom-call(f32[512,512]{1,0:T(8,128)S(1)} %get-tuple-element.57.w_in, f32[512,512]{1,0:T(8,128)S(1)} %get-tuple-element.58.l_in, f32[512,512]{1,0:T(8,128)S(1)} %get-tuple-element.59.i_in), custom_call_target="tpu_custom_call", output_to_operand_aliasing={{0}: (0, {}), {1}: (1, {}), {2}: (2, {})} | custom-call | flops 6000000000 | bytes 3145728 | tf_op jit(solution)/shard_map/pallas_call | solution.py:122
  93.7 0.0 copy-start.3
  93.8 1.0 copy-done.3
  94.7 0.6 constant_dynamic-slice_fusion
  95.3 0.9 collective-permute-done.11.far
  96.2 0.0 collective-permute-done.15.refs_6_
  96.2 0.0 collective-permute-done.18.refs_9_
  96.2 0.0 copy-start.4
  96.2 1.2 %copy-done.4 = f32[512,512]{1,0:T(8,128)S(1)} copy-done((f32[512,512]{1,0:T(8,128)S(1)}, f32[512,512]{1,0:T(8,128)}, u32[]{:S(2)}) %copy-start.4) | copy-done | bytes 1048600
  97.4 13.6 %shard_map.62 = (f32[12,4,4,2,32,128]{5,4,3,2,1,0:T(8,128)}, f32[192,512]{1,0:T(8,128)}) custom-call(s32[4]{0:T(128)S(1)} %pad_add_fusion.where, f32[512,512]{1,0:T(8,128)S(1)} %copy-done.4, f32[4,32,512]{2,1,0:T(8,128)S(1)} %pad_maximum_fusion.near, f32[4,32,512]{2,1,0:T(8,128)S(1)} %collective-permute-done.11.far, f32[192,512]{1,0:T(8,128)S(1)} %bitcast.20, ...), custom_call_target="tpu_custom_call" | custom-call | flops 5000000000 | bytes 27262976 | tf_op jit(solution)/shard_map/pallas_call | solution.py:241
  (27 shorter events, 0.1 us)
Async XLA Ops:
  0.6 26.8 %copy-start = (f32[12,1,1,16,512]{4,3,2,1,0:T(8,128)S(1)}, f32[12,1,1,16,512]{4,3,2,1,0:T(8,128)}, u32[]{:S(2)}) copy-start(f32[12,1,1,16,512]{4,3,2,1,0:T(8,128)} %param.4) | copy-start | bytes 1179652
  0.6 19.3 %collective-permute-start.1 = (f32[192,512]{1,0:T(8,128)}, f32[192,512]{1,0:T(8,128)S(1)}, u32[]{:S(2)}, u32[]{:S(2)}) collective-permute-start(f32[192,512]{1,0:T(8,128)} %bitcast.17), channel_id=1, source_target_pairs={{6,0},{25,1},{0,2},{27,3},{2,4},{29,5},{4,6},{31,7},{14,8},{1,9},{... | collective-permute-start | bytes 1179656 | tf_op jit(solution)/shard_map/ppermute | solution.py:268
  2.8 17.1 %collective-permute-start = (f32[192,512]{1,0:T(8,128)}, f32[192,512]{1,0:T(8,128)S(1)}, u32[]{:S(2)}, u32[]{:S(2)}) collective-permute-start(f32[192,512]{1,0:T(8,128)} %bitcast.18), channel_id=1, source_target_pairs={{2,0},{9,1},{4,2},{11,3},{6,4},{13,5},{0,6},{15,7},{10,8},{17,9},{... | collective-permute-start | bytes 1179656 | tf_op jit(solution)/shard_map/ppermute | solution.py:268
  19.9 11.6 %collective-permute-start.2 = (f32[96,512]{1,0:T(8,128)S(1)}, f32[96,512]{1,0:T(8,128)S(1)}, u32[]{:S(2)}, u32[]{:S(2)}) collective-permute-start(f32[96,512]{1,0:T(8,128)S(1)} %slice.38), channel_id=1, source_target_pairs={{6,0},{25,1},{0,2},{27,3},{2,4},{29,5},{4,6},{31,7},{14,8},{1,9},{... | collective-permute-start | bytes 589832 | tf_op jit(solution)/shard_map/ppermute | solution.py:268
  20.9 18.6 %all-to-all-start.1 = ((f32[16,8,8,128]{3,2,1,0:T(8,128)}), f32[16,8,8,128]{3,2,1,0:T(8,128)}, u32[]{:S(2)}, u32[]{:S(2)}) async-start(f32[16,8,8,128]{3,2,1,0:T(8,128)} %broadcast_in_dim.15), calls=%async_computation.1 | async-start | bytes 1048576 | tf_op jit(solution)/shard_map/all_to_all | solution.py:303
  28.2 9.7 %collective-permute-start.3 = (f32[96,512]{1,0:T(8,128)S(1)}, f32[96,512]{1,0:T(8,128)S(1)}, u32[]{:S(2)}, u32[]{:S(2)}) collective-permute-start(f32[96,512]{1,0:T(8,128)S(1)} %slice.39), channel_id=1, source_target_pairs={{2,0},{9,1},{4,2},{11,3},{6,4},{13,5},{0,6},{15,7},{10,8},{17,9},{... | collective-permute-start | bytes 589832 | tf_op jit(solution)/shard_map/ppermute | solution.py:268
  39.5 10.0 %collective-permute-start.4 = (f32[128,8,128]{2,1,0:T(8,128)}, f32[128,8,128]{2,1,0:T(8,128)}, u32[]{:S(2)}, u32[]{:S(2)}) collective-permute-start(f32[128,8,128]{2,1,0:T(8,128)} %bitcast.5.own_ref), channel_id=1, source_target_pairs={{1,0},{0,1},{3,2},{2,3},{5,4},{4,5},{7,6},{6,7},{9,8},{8,9},{11,10... | collective-permute-start | bytes 1572872 | tf_op jit(solution)/shard_map/ppermute | solution.py:268
  41.5 2.8 %collective-permute-start.5 = (f32[32,512]{1,0:T(8,128)}, f32[32,512]{1,0:T(8,128)}, u32[]{:S(2)}, u32[]{:S(2)}) collective-permute-start(f32[32,512]{1,0:T(8,128)} %bitcast.7), channel_id=1, source_target_pairs={{1,0},{0,1},{3,2},{2,3},{5,4},{4,5},{7,6},{6,7},{9,8},{8,9},{11,10... | collective-permute-start | bytes 196616 | tf_op jit(solution)/shard_map/ppermute | solution.py:268
  41.6 30.9 %collective-permute-start.9 = (f32[768,512]{1,0:T(8,128)}, f32[768,512]{1,0:T(8,128)S(1)}, u32[]{:S(2)}, u32[]{:S(2)}) collective-permute-start(f32[768,512]{1,0:T(8,128)} %constant_dynamic-update-slice_fusion.refs_0_), channel_id=1, source_target_pairs={{24,0},{7,1},{26,2},{1,3},{28,4},{3,5},{30,6},{5,7},{0,8},{15,9},{... | collective-permute-start | bytes 4718600 | tf_op jit(solution)/shard_map/ppermute | solution.py:268
  42.6 29.9 %collective-permute-start.8 = (f32[768,512]{1,0:T(8,128)}, f32[768,512]{1,0:T(8,128)S(1)}, u32[]{:S(2)}, u32[]{:S(2)}) collective-permute-start(f32[768,512]{1,0:T(8,128)} %constant_dynamic-update-slice_fusion.refs_0_), channel_id=1, source_target_pairs={{8,0},{3,1},{10,2},{5,3},{12,4},{7,5},{14,6},{1,7},{16,8},{11,9},{... | collective-permute-start | bytes 4718600 | tf_op jit(solution)/shard_map/ppermute | solution.py:268
  45.1 20.4 %collective-permute-start.6 = (f32[32,512]{1,0:T(8,128)S(1)}, f32[32,512]{1,0:T(8,128)S(1)}, u32[]{:S(2)}, u32[]{:S(2)}) collective-permute-start(f32[32,512]{1,0:T(8,128)S(1)} %pad_maximum_fusion.2), channel_id=1, source_target_pairs={{0,0},{16,1},{32,2},{48,3},{64,4},{80,5},{96,6},{112,7},{128,8},{1... | collective-permute-start | bytes 196616 | tf_op jit(solution)/shard_map/ppermute | solution.py:268
  49.3 39.1 %collective-permute-start.14 = (f32[768,512]{1,0:T(8,128)}, f32[768,512]{1,0:T(8,128)}, u32[]{:S(2)}, u32[]{:S(2)}) collective-permute-start(f32[768,512]{1,0:T(8,128)} %constant_dynamic-update-slice_fusion.refs_0_), channel_id=1, source_target_pairs={{1,0},{0,1},{3,2},{2,3},{5,4},{4,5},{7,6},{6,7},{9,8},{8,9},{11,10... | collective-permute-start | bytes 4718600 | tf_op jit(solution)/shard_map/ppermute | solution.py:268
  65.5 7.0 %collective-permute-start.7 = (f32[1,32,512]{2,1,0:T(8,128)S(1)}, f32[1,32,512]{2,1,0:T(8,128)S(1)}, u32[]{:S(2)}, u32[]{:S(2)}) collective-permute-start(f32[1,32,512]{2,1,0:T(8,128)S(1)} %bitcast.22), channel_id=1, source_target_pairs={{128,0},{129,1},{130,2},{131,3},{132,4},{133,5},{134,6},{135,7},{1... | collective-permute-start | bytes 196616 | tf_op jit(solution)/shard_map/ppermute | solution.py:268
  71.2 3.3 %copy-start.1 = (f32[512,512]{1,0:T(8,128)}, f32[512,512]{1,0:T(8,128)S(1)}, u32[]{:S(2)}) copy-start(f32[512,512]{1,0:T(8,128)S(1)} %get-tuple-element.52.i_in) | copy-start | bytes 3145732
  71.2 3.3 %copy-start.5 = (f32[512,512]{1,0:T(8,128)}, f32[512,512]{1,0:T(8,128)S(1)}, u32[]{:S(2)}) copy-start(f32[512,512]{1,0:T(8,128)S(1)} %get-tuple-element.51.l_in) | copy-start | bytes 3145732
  71.2 3.3 %copy-start.7 = (f32[512,512]{1,0:T(8,128)}, f32[512,512]{1,0:T(8,128)S(1)}, u32[]{:S(2)}) copy-start(f32[512,512]{1,0:T(8,128)S(1)} %get-tuple-element.50.w_in) | copy-start | bytes 3145732
  72.5 2.0 %copy-start.9 = (f32[2,32,512]{2,1,0:T(8,128)}, f32[2,32,512]{2,1,0:T(8,128)S(1)}, u32[]{:S(2)}) copy-start(f32[2,32,512]{2,1,0:T(8,128)S(1)} %pad_maximum_fusion.1) | copy-start | bytes 393220
  72.5 5.3 %collective-permute-start.10 = (f32[2,32,512]{2,1,0:T(8,128)S(1)}, f32[2,32,512]{2,1,0:T(8,128)S(1)}, u32[]{:S(2)}, u32[]{:S(2)}) collective-permute-start(f32[2,32,512]{2,1,0:T(8,128)S(1)} %pad_maximum_fusion.1), channel_id=1, source_target_pairs={{64,0},{65,1},{66,2},{67,3},{68,4},{69,5},{70,6},{71,7},{72,8},{73... | collective-permute-start | bytes 393224 | tf_op jit(solution)/shard_map/ppermute | solution.py:268
  73.6 14.1 %collective-permute-start.12 = (f32[384,512]{1,0:T(8,128)}, f32[384,512]{1,0:T(8,128)}, u32[]{:S(2)}, u32[]{:S(2)}) collective-permute-start(f32[384,512]{1,0:T(8,128)} %slice.48), channel_id=1, source_target_pairs={{24,0},{7,1},{26,2},{1,3},{28,4},{3,5},{30,6},{5,7},{0,8},{15,9},{... | collective-permute-start | bytes 2359304 | tf_op jit(solution)/shard_map/ppermute | solution.py:268
  74.5 13.7 %collective-permute-start.13 = (f32[384,512]{1,0:T(8,128)}, f32[384,512]{1,0:T(8,128)}, u32[]{:S(2)}, u32[]{:S(2)}) collective-permute-start(f32[384,512]{1,0:T(8,128)} %slice.49), channel_id=1, source_target_pairs={{8,0},{3,1},{10,2},{5,3},{12,4},{7,5},{14,6},{1,7},{16,8},{11,9},{... | collective-permute-start | bytes 2359304 | tf_op jit(solution)/shard_map/ppermute | solution.py:268
  77.2 18.9 %collective-permute-start.15 = (f32[768,512]{1,0:T(8,128)S(1)}, f32[768,512]{1,0:T(8,128)}, u32[]{:S(2)}, u32[]{:S(2)}) collective-permute-start(f32[768,512]{1,0:T(8,128)S(1)} %collective-permute-done.8.refs_1_), channel_id=1, source_target_pairs={{1,0},{0,1},{3,2},{2,3},{5,4},{4,5},{7,6},{6,7},{9,8},{8,9},{11,10... | collective-permute-start | bytes 4718600 | tf_op jit(solution)/shard_map/ppermute | solution.py:268
  77.9 0.7 copy-start.11
  78.5 17.7 %collective-permute-start.18 = (f32[768,512]{1,0:T(8,128)S(1)}, f32[768,512]{1,0:T(8,128)}, u32[]{:S(2)}, u32[]{:S(2)}) collective-permute-start(f32[768,512]{1,0:T(8,128)S(1)} %collective-permute-done.9.refs_4_), channel_id=1, source_target_pairs={{1,0},{0,1},{3,2},{2,3},{5,4},{4,5},{7,6},{6,7},{9,8},{8,9},{11,10... | collective-permute-start | bytes 4718600 | tf_op jit(solution)/shard_map/ppermute | solution.py:268
  78.5 1.2 %copy-start.2 = (f32[512,512]{1,0:T(8,128)S(1)}, f32[512,512]{1,0:T(8,128)}, u32[]{:S(2)}) copy-start(f32[512,512]{1,0:T(8,128)} %copy-done.1) | copy-start | bytes 3145732
  79.8 1.2 %copy-start.6 = (f32[512,512]{1,0:T(8,128)S(1)}, f32[512,512]{1,0:T(8,128)}, u32[]{:S(2)}) copy-start(f32[512,512]{1,0:T(8,128)} %copy-done.5) | copy-start | bytes 3145732
  81.0 1.2 %copy-start.8 = (f32[512,512]{1,0:T(8,128)S(1)}, f32[512,512]{1,0:T(8,128)}, u32[]{:S(2)}) copy-start(f32[512,512]{1,0:T(8,128)} %copy-done.7) | copy-start | bytes 3145732
  82.2 6.2 %copy-start.10 = (f32[2,32,512]{2,1,0:T(8,128)S(1)}, f32[2,32,512]{2,1,0:T(8,128)}, u32[]{:S(2)}) copy-start(f32[2,32,512]{2,1,0:T(8,128)} %copy-done.9) | copy-start | bytes 393220
  82.2 6.2 %copy-start.12 = (f32[2,32,512]{2,1,0:T(8,128)S(1)}, f32[2,32,512]{2,1,0:T(8,128)}, u32[]{:S(2)}) copy-start(f32[2,32,512]{2,1,0:T(8,128)} %copy-done.11) | copy-start | bytes 393220
  87.6 8.5 %collective-permute-start.16 = (f32[384,512]{1,0:T(8,128)}, f32[384,512]{1,0:T(8,128)S(1)}, u32[]{:S(2)}, u32[]{:S(2)}) collective-permute-start(f32[384,512]{1,0:T(8,128)} %collective-permute-done.12.refs_2_), channel_id=1, source_target_pairs={{1,0},{0,1},{3,2},{2,3},{5,4},{4,5},{7,6},{6,7},{9,8},{8,9},{11,10... | collective-permute-start | bytes 2359304 | tf_op jit(solution)/shard_map/ppermute | solution.py:268
  88.2 7.9 %collective-permute-start.17 = (f32[384,512]{1,0:T(8,128)}, f32[384,512]{1,0:T(8,128)S(1)}, u32[]{:S(2)}, u32[]{:S(2)}) collective-permute-start(f32[384,512]{1,0:T(8,128)} %collective-permute-done.13.refs_3_), channel_id=1, source_target_pairs={{1,0},{0,1},{3,2},{2,3},{5,4},{4,5},{7,6},{6,7},{9,8},{8,9},{11,10... | collective-permute-start | bytes 2359304 | tf_op jit(solution)/shard_map/ppermute | solution.py:268
  88.4 7.8 %collective-permute-start.11 = (f32[4,32,512]{2,1,0:T(8,128)S(1)}, f32[4,32,512]{2,1,0:T(8,128)S(1)}, u32[]{:S(2)}, u32[]{:S(2)}) collective-permute-start(f32[4,32,512]{2,1,0:T(8,128)S(1)} %pad_maximum_fusion.near), channel_id=1, source_target_pairs={{32,0},{33,1},{34,2},{35,3},{36,4},{37,5},{38,6},{39,7},{40,8},{41... | collective-permute-start | bytes 786440 | tf_op jit(solution)/shard_map/ppermute | solution.py:268
  93.7 1.0 copy-start.3
  96.2 1.2 %copy-start.4 = (f32[512,512]{1,0:T(8,128)S(1)}, f32[512,512]{1,0:T(8,128)}, u32[]{:S(2)}) copy-start(f32[512,512]{1,0:T(8,128)} %copy-done.3) | copy-start | bytes 3145732

commit v2 on v1

--- a/solution.py
+++ b/solution.py
@@ -16,12 +16,6 @@
 
 def dot(a, b):
     return jnp.dot(a, b, precision=lax.Precision.HIGHEST, preferred_element_type=F32)
-
-
-def dot_t(a, b):
-    return lax.dot_general(
-        a, b, (((1,), (1,)), ((), ())), precision=lax.Precision.HIGHEST, preferred_element_type=F32
-    )
 
 
 def row(v, j):
@@ -110,7 +104,7 @@
         in_specs=[SMEM, VMEM, VMEM],
         out_specs=(VMEM,) * 3,
         scratch_shapes=[pltpu.VMEM((order * order // 128, 128), F32)],
-        compiler_params=pltpu.CompilerParams(vmem_limit_bytes=16 << 20),
+        compiler_params=pltpu.CompilerParams(vmem_limit_bytes=12 << 20),
         cost_estimate=pl.CostEstimate(flops=6_000_000_000, bytes_accessed=3 << 20, transcendentals=0),
     )(where, own, other)
 
@@ -125,7 +119,7 @@
         in_specs=[VMEM] * 3,
         out_specs=(VMEM,) * 3,
         input_output_aliases={0: 0, 1: 1, 2: 2},
-        compiler_params=pltpu.CompilerParams(vmem_limit_bytes=16 << 20),
+        compiler_params=pltpu.CompilerParams(vmem_limit_bytes=12 << 20),
         cost_estimate=pl.CostEstimate(flops=6_000_000_000, bytes_accessed=3 << 20, transcendentals=0),
     )(*state)
 
@@ -138,9 +132,9 @@
     return hi, (v - hi.astype(F32)).astype(BF16)
 
 
-def dot3(a, b):
+def dot3(a, b, dim=0):
     def one(p, q):
-        return jnp.dot(p, q, preferred_element_type=F32)
+        return lax.dot_general(p, q, (((1,), (dim,)), ((), ())), preferred_element_type=F32)
 
     return one(a[0], b[0]) + (one(a[0], b[1]) + one(a[1], b[0]))
 
@@ -191,9 +185,10 @@
         v = near[n] if n < NZ // 2 else far[n - NZ // 2]
         bits = n % 2 * 4 + n // 2 % 2 * 2 + n // 4
         win[pl.ds(pl.multiple_of((where[0] ^ bits) * part, part), part), :] = v
-    g = dot_t(win[...], inv[...])
-    mine_ref[...] = dot_t(own[...], inv[...])
-    w = dot(g, inv[...]).T
+    inverse = split(inv[...])
+    g = dot3(split(win[...]), inverse, 1)
+    mine_ref[...] = dot3(split(own[...]), inverse, 1)
+    w = dot3(split(g), inverse, 0).T
     whi[...], wlo[...] = split(w)
 
     @pl.loop(0, count)
@@ -254,7 +249,7 @@
             pltpu.SemaphoreType.DMA((SLOTS, NX)),
             pltpu.SemaphoreType.DMA((SLOTS, NX)),
         ],
-        compiler_params=pltpu.CompilerParams(vmem_limit_bytes=40 << 20),
+        compiler_params=pltpu.CompilerParams(vmem_limit_bytes=14 << 20),
         cost_estimate=pl.CostEstimate(flops=5_000_000_000, bytes_accessed=26 << 20, transcendentals=0),
     )(where, inv, *window, own, *flat, slab)
 
@@ -292,11 +287,14 @@
     return along(phase, lambda i: (i + 3) % 4)
 
 
-def scatter(v, rows):
+def chip_rows(v, rows):
     core = lax.axis_index("core")
     got = other_core(v)
-    sent = jnp.concatenate([jnp.where(core == 0, v[:rows], got[rows:]), jnp.where(core == 0, got[:rows], v[rows:])], 0)
-    return receive(sent, lambda z, y, x, c: (y % 2 * NX + x, 2 * c + z // NX, z % NX, y // 2))
+    return jnp.concatenate([jnp.where(core == 0, v[:rows], got[rows:]), jnp.where(core == 0, got[:rows], v[rows:])], 0)
+
+
+def from_owner(v):
+    return receive(v, lambda z, y, x, c: (y % 2 * NX + x, 2 * c + z // NX, z % NX, y // 2))
 
 
 def everyone(v, axis, size):
@@ -320,12 +318,13 @@
 
     up, down = receive(p, plus(0)), receive(p, minus(0))
     d = everyone(diag_block.reshape(8, 128), "z", NZ)
-    d, up, down = tie((d, up, down))
+    w = chip_rows(p[: 2 * rb], rb)
+    d, up, down, w = tie((d, up, down, w))
     first, second = forward(up, down, 0)
     block = jnp.concatenate([p, up, first, second, down], 0)
     d = everyone(d, ("y", "x"), NY * NX).reshape(-1, 8, 128)
-    w = scatter(p[: 2 * rb], rb).reshape(1, 2 * rb, order)
-    d, block = tie((d, block))
+    w = from_owner(w).reshape(1, 2 * rb, order)
+    d, block, w = tie((d, block, w))
     up, down = receive(block, plus(1)), receive(block, minus(1))
     state = factor_first(where, d, other_core(d), order)
     for t, bit in ((1, 4), (2, 2), (3, 1)):

time: 112 us -> 112 us (level); the launches traced: 111 us -> 110 us
  starting transfers between devices: 25.3 us -> 46.6 us
  blocking collectives: 14.8 us -> 0 us
  waiting for transfers between devices: 17.2 us -> 9.15 us
  local copies, waits for them, and re-layouts: 14.9 us -> 16.4 us
    all_to_all x1 -> x0, blocking collectives: 14.8 us -> none  [everyone(): lax.all_to_all(jnp.broadcast_to(v[None], (size, *v.shape)), axis, 0, 0, t...]
    ppermute x19, starting transfers between devices: 18.8 us -> 33.3 us  [receive(): lax.ppermute(v, ALL, [(index(*source(*at)), index(*at)) for at in places])]
    ppermute x19, waiting for transfers between devices: 17.2 us -> 3.08 us  [receive(): lax.ppermute(v, ALL, [(index(*source(*at)), index(*at)) for at in places])]
    all_to_all x1 -> x2, starting transfers between devices: 6.51 us -> 13.3 us  [everyone(): lax.all_to_all(jnp.broadcast_to(v[None], (size, *v.shape)), axis, 0, 0, t...]
    all_to_all x1 -> x2, waiting for transfers between devices: 0.01 us -> 6.07 us  [everyone(): lax.all_to_all(jnp.broadcast_to(v[None], (size, *v.shape)), axis, 0, 0, t...]
    unnamed x30 -> x38, local copies, waits for them, and re-layouts: 9.49 us -> 10 us
  transfers between devices with their start and end apart: 20 -> 21, of which waited for: 5 -> 2; matrix products, arithmetic and copies ran while one was open for 8% -> 8% of each run, Pallas kernels for 21% -> 21%
where the time goes in v2:
time: 112 us; the launch traced here: 110 us
  starting transfers between devices  46.6 us (42%)
  Pallas kernels  35.9 us (32%)
  local copies, waits for them, and re-layouts  16.4 us (15%)
  waiting for transfers between devices  9.15 us (8%)
    ppermute x19, starting transfers between devices, receive(): lax.ppermute(v, ALL, [(index(*source(*at)), index(*at)) for at in places])  33.3 us
    pallas_call x3, Pallas kernels, factor_next(): pl.pallas_call(body, out_shape=tuple((jax.ShapeDtypeStruct(a.shape, F32)...  16.1 us
    all_to_all x2, starting transfers between devices, everyone(): lax.all_to_all(jnp.broadcast_to(v[None], (size, *v.shape)), axis, 0, 0, t...  13.3 us
    pallas_call x1, Pallas kernels, update(): pl.pallas_call(body, out_shape=(jax.ShapeDtypeStruct(slab.shape, F32), ja...  12.5 us
    unnamed x38, local copies, waits for them, and re-layouts  10 us
    pallas_call x1, Pallas kernels, factor_first(): pl.pallas_call(first_kernel, out_shape=(shape,) * 3, in_specs=[SMEM, VMEM...  7.27 us
    all_to_all x2, waiting for transfers between devices, everyone(): lax.all_to_all(jnp.broadcast_to(v[None], (size, *v.shape)), axis, 0, 0, t...  6.07 us
    ppermute x19, waiting for transfers between devices, receive(): lax.ppermute(v, ALL, [(index(*source(*at)), index(*at)) for at in places])  3.08 us
  transfers between devices with their start and end apart: 21, of which 2 were waited for; matrix products, arithmetic and copies ran while one was open for 8% of the time, Pallas kernels for 21%

profile of v2, /device:TPU:1, one launch (start us, length us, event | category | flops | bytes accessed | tf_op | source)
XLA Modules:
  0.0 110.0 jit_solution(3701690998916983681)
XLA Ops:
  0.6 0.0 copy-start
  0.6 0.9 slice.40
  1.6 3.2 %collective-permute-start.2 = (f32[32,512]{1,0:T(8,128)S(1)}, f32[32,512]{1,0:T(8,128)S(1)}, u32[]{:S(2)}, u32[]{:S(2)}) collective-permute-start(f32[32,512]{1,0:T(8,128)S(1)} %bitcast.24), channel_id=1, source_target_pairs={{1,0},{0,1},{3,2},{2,3},{5,4},{4,5},{7,6},{6,7},{9,8},{8,9},{11,10... | collective-permute-start | bytes 196616 | tf_op jit(solution)/shard_map/ppermute | solution.py:263
  4.8 0.0 collective-permute-start.1
  4.8 2.7 %collective-permute-start = (f32[192,512]{1,0:T(8,128)}, f32[192,512]{1,0:T(8,128)S(1)}, u32[]{:S(2)}, u32[]{:S(2)}) collective-permute-start(f32[192,512]{1,0:T(8,128)} %bitcast.21), channel_id=1, source_target_pairs={{2,0},{9,1},{4,2},{11,3},{6,4},{13,5},{0,6},{15,7},{10,8},{17,9},{... | collective-permute-start | bytes 1179656 | tf_op jit(solution)/shard_map/ppermute | solution.py:263
  7.5 0.7 broadcast_in_dim.6
  8.2 0.6 broadcast_in_dim.14
  8.8 6.5 %all-to-all-start = ((f32[8,8,128]{2,1,0:T(8,128)}), f32[8,8,128]{2,1,0:T(8,128)S(1)}, u32[]{:S(2)}, u32[]{:S(2)}) async-start(f32[8,8,128]{2,1,0:T(8,128)} %broadcast_in_dim.14), calls=%async_computation | async-start | bytes 65536 | tf_op jit(solution)/shard_map/all_to_all | solution.py:301
  15.3 0.8 slice_select_fusion.1
  16.1 6.1 %all-to-all-done = f32[8,8,128]{2,1,0:T(8,128)S(1)} async-done(((f32[8,8,128]{2,1,0:T(8,128)}), f32[8,8,128]{2,1,0:T(8,128)S(1)}, u32[]{:S(2)}, u32[]{:S(2)}) %all-to-all-start) | async-done | bytes 32800 | tf_op jit(solution)/shard_map/all_to_all | solution.py:301
  22.2 0.0 collective-permute-done.1
  22.2 0.0 collective-permute-done
  22.2 0.1 collective-permute-start.3
  22.3 0.8 broadcast_in_dim.15
  23.1 6.8 %all-to-all-start.1 = ((f32[16,8,8,128]{3,2,1,0:T(8,128)}), f32[16,8,8,128]{3,2,1,0:T(8,128)}, u32[]{:S(2)}, u32[]{:S(2)}) async-start(f32[16,8,8,128]{3,2,1,0:T(8,128)} %broadcast_in_dim.15), calls=%async_computation.1 | async-start | bytes 1048576 | tf_op jit(solution)/shard_map/all_to_all | solution.py:301
  30.0 0.8 constant_dynamic-update-slice_fusion.4
  30.8 7.4 %collective-permute-start.5 = (f32[32,512]{1,0:T(8,128)S(1)}, f32[32,512]{1,0:T(8,128)S(1)}, u32[]{:S(2)}, u32[]{:S(2)}) collective-permute-start(f32[32,512]{1,0:T(8,128)S(1)} %pad_maximum_fusion.2), channel_id=1, source_target_pairs={{0,0},{16,1},{32,2},{48,3},{64,4},{80,5},{96,6},{112,7},{128,8},{1... | collective-permute-start | bytes 196616 | tf_op jit(solution)/shard_map/ppermute | solution.py:263
  38.2 0.1 collective-permute-start.4
  38.2 0.8 constant_dynamic-update-slice_fusion.3
  39.0 0.7 constant_dynamic-update-slice_fusion.2
  39.7 3.0 %collective-permute-done.4 = f32[96,512]{1,0:T(8,128)S(1)} collective-permute-done((f32[96,512]{1,0:T(8,128)S(1)}, f32[96,512]{1,0:T(8,128)S(1)}, u32[]{:S(2)}, u32[]{:S(2)}) %collective-permute-start.4) | collective-permute-done | bytes 196640 | tf_op jit(solution)/shard_map/ppermute | solution.py:263
  42.8 0.7 constant_dynamic-update-slice_fusion.1
  43.4 0.8 constant_dynamic-update-slice_fusion.refs_0_
  44.2 0.0 collective-permute-done.5
  44.2 0.1 collective-permute-start.6
  44.3 0.5 copy-done.13
  44.9 1.2 %collective-permute-start.9 = (f32[768,512]{1,0:T(8,128)}, f32[768,512]{1,0:T(8,128)S(1)}, u32[]{:S(2)}, u32[]{:S(2)}) collective-permute-start(f32[768,512]{1,0:T(8,128)} %constant_dynamic-update-slice_fusion.refs_0_), channel_id=1, source_target_pairs={{24,0},{7,1},{26,2},{1,3},{28,4},{3,5},{30,6},{5,7},{0,8},{15,9},{... | collective-permute-start | bytes 4718600 | tf_op jit(solution)/shard_map/ppermute | solution.py:263
  46.0 1.5 %collective-permute-start.8 = (f32[768,512]{1,0:T(8,128)}, f32[768,512]{1,0:T(8,128)S(1)}, u32[]{:S(2)}, u32[]{:S(2)}) collective-permute-start(f32[768,512]{1,0:T(8,128)} %constant_dynamic-update-slice_fusion.refs_0_), channel_id=1, source_target_pairs={{8,0},{3,1},{10,2},{5,3},{12,4},{7,5},{14,6},{1,7},{16,8},{11,9},{... | collective-permute-start | bytes 4718600 | tf_op jit(solution)/shard_map/ppermute | solution.py:263
  47.5 0.1 pad_add_fusion.where
  47.6 1.4 %collective-permute-start.14 = (f32[768,512]{1,0:T(8,128)}, f32[768,512]{1,0:T(8,128)}, u32[]{:S(2)}, u32[]{:S(2)}) collective-permute-start(f32[768,512]{1,0:T(8,128)} %constant_dynamic-update-slice_fusion.refs_0_), channel_id=1, source_target_pairs={{1,0},{0,1},{3,2},{2,3},{5,4},{4,5},{7,6},{6,7},{9,8},{8,9},{11,10... | collective-permute-start | bytes 4718600 | tf_op jit(solution)/shard_map/ppermute | solution.py:263
  49.0 0.0 collective-permute-done.6.other_ref
  49.0 7.3 %shard_map.58 = (f32[512,512]{1,0:T(8,128)S(1)}, f32[512,512]{1,0:T(8,128)S(1)}, f32[512,512]{1,0:T(8,128)S(1)}) custom-call(s32[4]{0:T(128)S(1)} %pad_add_fusion.where, f32[128,8,128]{2,1,0:T(8,128)} %bitcast.8.own_ref, f32[128,8,128]{2,1,0:T(8,128)} %collective-permute-done.6.other_ref), custom_call_target="tpu_custom_call" | custom-call | flops 6000000000 | bytes 3145728 | tf_op jit(solution)/shard_map/pallas_call | solution.py:101
  56.3 4.6 %collective-permute-start.7 = (f32[1,32,512]{2,1,0:T(8,128)S(1)}, f32[1,32,512]{2,1,0:T(8,128)S(1)}, u32[]{:S(2)}, u32[]{:S(2)}) collective-permute-start(f32[1,32,512]{2,1,0:T(8,128)S(1)} %bitcast.25), channel_id=1, source_target_pairs={{128,0},{129,1},{130,2},{131,3},{132,4},{133,5},{134,6},{135,7},{1... | collective-permute-start | bytes 196616 | tf_op jit(solution)/shard_map/ppermute | solution.py:263
  60.9 5.7 %shard_map.59 = (f32[512,512]{1,0:T(8,128)S(1)}, f32[512,512]{1,0:T(8,128)S(1)}, f32[512,512]{1,0:T(8,128)S(1)}) custom-call(f32[512,512]{1,0:T(8,128)S(1)} %get-tuple-element.46.w_in, f32[512,512]{1,0:T(8,128)S(1)} %get-tuple-element.47.l_in, f32[512,512]{1,0:T(8,128)S(1)} %get-tuple-element.48.i_in), custom_call_target="tpu_custom_call", output_to_operand_aliasing={{0}: (0, {}), {1}: (1, {}), {2}: (2, {})} | custom-call | flops 6000000000 | bytes 3145728 | tf_op jit(solution)/shard_map/pallas_call | solution.py:116
  66.6 0.0 copy-start.7
  66.6 0.0 collective-permute-done.7
  66.7 0.0 collective-permute-done.8.refs_1_
  66.7 3.6 %collective-permute-start.10 = (f32[2,32,512]{2,1,0:T(8,128)S(1)}, f32[2,32,512]{2,1,0:T(8,128)S(1)}, u32[]{:S(2)}, u32[]{:S(2)}) collective-permute-start(f32[2,32,512]{2,1,0:T(8,128)S(1)} %pad_maximum_fusion.1), channel_id=1, source_target_pairs={{64,0},{65,1},{66,2},{67,3},{68,4},{69,5},{70,6},{71,7},{72,8},{73... | collective-permute-start | bytes 393224 | tf_op jit(solution)/shard_map/ppermute | solution.py:263
  70.3 0.9 slice.48
  71.3 0.0 collective-permute-start.12
  71.3 0.9 slice.49
  72.2 2.8 %collective-permute-start.13 = (f32[384,512]{1,0:T(8,128)}, f32[384,512]{1,0:T(8,128)}, u32[]{:S(2)}, u32[]{:S(2)}) collective-permute-start(f32[384,512]{1,0:T(8,128)} %slice.49), channel_id=1, source_target_pairs={{8,0},{3,1},{10,2},{5,3},{12,4},{7,5},{14,6},{1,7},{16,8},{11,9},{... | collective-permute-start | bytes 2359304 | tf_op jit(solution)/shard_map/ppermute | solution.py:263
  75.0 1.7 %collective-permute-start.15 = (f32[768,512]{1,0:T(8,128)S(1)}, f32[768,512]{1,0:T(8,128)}, u32[]{:S(2)}, u32[]{:S(2)}) collective-permute-start(f32[768,512]{1,0:T(8,128)S(1)} %collective-permute-done.8.refs_1_), channel_id=1, source_target_pairs={{1,0},{0,1},{3,2},{2,3},{5,4},{4,5},{7,6},{6,7},{9,8},{8,9},{11,10... | collective-permute-start | bytes 4718600 | tf_op jit(solution)/shard_map/ppermute | solution.py:263
  76.6 0.0 collective-permute-done.10
  76.6 0.7 copy-done.11
  77.3 0.0 collective-permute-start.18
  77.3 1.2 %copy-done.2 = f32[512,512]{1,0:T(8,128)S(1)} copy-done((f32[512,512]{1,0:T(8,128)S(1)}, f32[512,512]{1,0:T(8,128)}, u32[]{:S(2)}) %copy-start.2) | copy-done | bytes 1048600
  78.5 1.2 %copy-done.6 = f32[512,512]{1,0:T(8,128)S(1)} copy-done((f32[512,512]{1,0:T(8,128)S(1)}, f32[512,512]{1,0:T(8,128)}, u32[]{:S(2)}) %copy-start.6) | copy-done | bytes 1048600
  79.8 1.2 %copy-done.8 = f32[512,512]{1,0:T(8,128)S(1)} copy-done((f32[512,512]{1,0:T(8,128)S(1)}, f32[512,512]{1,0:T(8,128)}, u32[]{:S(2)}) %copy-start.8) | copy-done | bytes 1048600
  81.0 5.4 %shard_map.60 = (f32[512,512]{1,0:T(8,128)S(1)}, f32[512,512]{1,0:T(8,128)S(1)}, f32[512,512]{1,0:T(8,128)S(1)}) custom-call(f32[512,512]{1,0:T(8,128)S(1)} %copy-done.8, f32[512,512]{1,0:T(8,128)S(1)} %copy-done.6, f32[512,512]{1,0:T(8,128)S(1)} %copy-done.2), custom_call_target="tpu_custom_call", output_to_operand_aliasing={{0}: (0, {}), {1}: (1, {}), {2}: (2, {})} | custom-call | flops 6000000000 | bytes 3145728 | tf_op jit(solution)/shard_map/pallas_call | solution.py:116
  86.4 0.0 collective-permute-done.12.refs_2_
  86.4 0.6 collective-permute-start.16
  87.0 0.0 collective-permute-done.13.refs_3_
  87.0 0.1 collective-permute-start.17
  87.1 0.0 slice-start
  87.2 2.3 %collective-permute-start.11 = (f32[4,32,512]{2,1,0:T(8,128)S(1)}, f32[4,32,512]{2,1,0:T(8,128)S(1)}, u32[]{:S(2)}, u32[]{:S(2)}) collective-permute-start(f32[4,32,512]{2,1,0:T(8,128)S(1)} %pad_maximum_fusion.near), channel_id=1, source_target_pairs={{32,0},{33,1},{34,2},{35,3},{36,4},{37,5},{38,6},{39,7},{40,8},{41... | collective-permute-start | bytes 786440 | tf_op jit(solution)/shard_map/ppermute | solution.py:263
  89.5 5.0 %shard_map.61 = (f32[512,512]{1,0:T(8,128)S(1)}, f32[512,512]{1,0:T(8,128)S(1)}, f32[512,512]{1,0:T(8,128)S(1)}) custom-call(f32[512,512]{1,0:T(8,128)S(1)} %get-tuple-element.61.w_in, f32[512,512]{1,0:T(8,128)S(1)} %get-tuple-element.62.l_in, f32[512,512]{1,0:T(8,128)S(1)} %get-tuple-element.63.i_in), custom_call_target="tpu_custom_call", output_to_operand_aliasing={{0}: (0, {}), {1}: (1, {}), {2}: (2, {})} | custom-call | flops 6000000000 | bytes 3145728 | tf_op jit(solution)/shard_map/pallas_call | solution.py:116
  94.4 0.0 copy-start.3
  94.5 1.0 copy-done.3
  95.4 0.6 constant_dynamic-slice_fusion
  96.0 0.0 collective-permute-done.11.far
  96.1 0.0 copy-start.4
  96.1 1.2 %copy-done.4 = f32[512,512]{1,0:T(8,128)S(1)} copy-done((f32[512,512]{1,0:T(8,128)S(1)}, f32[512,512]{1,0:T(8,128)}, u32[]{:S(2)}) %copy-start.4) | copy-done | bytes 1048600
  97.3 12.5 %shard_map.62 = (f32[12,4,4,2,32,128]{5,4,3,2,1,0:T(8,128)}, f32[192,512]{1,0:T(8,128)}) custom-call(s32[4]{0:T(128)S(1)} %pad_add_fusion.where, f32[512,512]{1,0:T(8,128)S(1)} %copy-done.4, f32[4,32,512]{2,1,0:T(8,128)S(1)} %pad_maximum_fusion.near, f32[4,32,512]{2,1,0:T(8,128)S(1)} %collective-permute-done.11.far, f32[192,512]{1,0:T(8,128)S(1)} %bitcast.23, ...), custom_call_target="tpu_custom_call" | custom-call | flops 5000000000 | bytes 27262976 | tf_op jit(solution)/shard_map/pallas_call | solution.py:236
  (37 shorter events, 0.1 us)
Async XLA Ops:
  0.6 29.3 %copy-start = (f32[12,1,1,16,512]{4,3,2,1,0:T(8,128)S(1)}, f32[12,1,1,16,512]{4,3,2,1,0:T(8,128)}, u32[]{:S(2)}) copy-start(f32[12,1,1,16,512]{4,3,2,1,0:T(8,128)} %param.4) | copy-start | bytes 1179652
  1.6 13.7 %collective-permute-start.2 = (f32[32,512]{1,0:T(8,128)S(1)}, f32[32,512]{1,0:T(8,128)S(1)}, u32[]{:S(2)}, u32[]{:S(2)}) collective-permute-start(f32[32,512]{1,0:T(8,128)S(1)} %bitcast.24), channel_id=1, source_target_pairs={{1,0},{0,1},{3,2},{2,3},{5,4},{4,5},{7,6},{6,7},{9,8},{8,9},{11,10... | collective-permute-start | bytes 196616 | tf_op jit(solution)/shard_map/ppermute | solution.py:263
  4.8 17.4 %collective-permute-start.1 = (f32[192,512]{1,0:T(8,128)}, f32[192,512]{1,0:T(8,128)S(1)}, u32[]{:S(2)}, u32[]{:S(2)}) collective-permute-start(f32[192,512]{1,0:T(8,128)} %bitcast.20), channel_id=1, source_target_pairs={{6,0},{25,1},{0,2},{27,3},{2,4},{29,5},{4,6},{31,7},{14,8},{1,9},{... | collective-permute-start | bytes 1179656 | tf_op jit(solution)/shard_map/ppermute | solution.py:263
  4.8 17.4 %collective-permute-start = (f32[192,512]{1,0:T(8,128)}, f32[192,512]{1,0:T(8,128)S(1)}, u32[]{:S(2)}, u32[]{:S(2)}) collective-permute-start(f32[192,512]{1,0:T(8,128)} %bitcast.21), channel_id=1, source_target_pairs={{2,0},{9,1},{4,2},{11,3},{6,4},{13,5},{0,6},{15,7},{10,8},{17,9},{... | collective-permute-start | bytes 1179656 | tf_op jit(solution)/shard_map/ppermute | solution.py:263
  8.8 13.4 %all-to-all-start = ((f32[8,8,128]{2,1,0:T(8,128)}), f32[8,8,128]{2,1,0:T(8,128)S(1)}, u32[]{:S(2)}, u32[]{:S(2)}) async-start(f32[8,8,128]{2,1,0:T(8,128)} %broadcast_in_dim.14), calls=%async_computation | async-start | bytes 65536 | tf_op jit(solution)/shard_map/all_to_all | solution.py:301
  22.2 16.8 %collective-permute-start.3 = (f32[96,512]{1,0:T(8,128)S(1)}, f32[96,512]{1,0:T(8,128)S(1)}, u32[]{:S(2)}, u32[]{:S(2)}) collective-permute-start(f32[96,512]{1,0:T(8,128)S(1)} %slice.46), channel_id=1, source_target_pairs={{6,0},{25,1},{0,2},{27,3},{2,4},{29,5},{4,6},{31,7},{14,8},{1,9},{... | collective-permute-start | bytes 589832 | tf_op jit(solution)/shard_map/ppermute | solution.py:263
  23.1 21.1 %all-to-all-start.1 = ((f32[16,8,8,128]{3,2,1,0:T(8,128)}), f32[16,8,8,128]{3,2,1,0:T(8,128)}, u32[]{:S(2)}, u32[]{:S(2)}) async-start(f32[16,8,8,128]{3,2,1,0:T(8,128)} %broadcast_in_dim.15), calls=%async_computation.1 | async-start | bytes 1048576 | tf_op jit(solution)/shard_map/all_to_all | solution.py:301
  30.8 13.5 %collective-permute-start.5 = (f32[32,512]{1,0:T(8,128)S(1)}, f32[32,512]{1,0:T(8,128)S(1)}, u32[]{:S(2)}, u32[]{:S(2)}) collective-permute-start(f32[32,512]{1,0:T(8,128)S(1)} %pad_maximum_fusion.2), channel_id=1, source_target_pairs={{0,0},{16,1},{32,2},{48,3},{64,4},{80,5},{96,6},{112,7},{128,8},{1... | collective-permute-start | bytes 196616 | tf_op jit(solution)/shard_map/ppermute | solution.py:263
  38.2 4.6 %collective-permute-start.4 = (f32[96,512]{1,0:T(8,128)S(1)}, f32[96,512]{1,0:T(8,128)S(1)}, u32[]{:S(2)}, u32[]{:S(2)}) collective-permute-start(f32[96,512]{1,0:T(8,128)S(1)} %slice.47), channel_id=1, source_target_pairs={{2,0},{9,1},{4,2},{11,3},{6,4},{13,5},{0,6},{15,7},{10,8},{17,9},{... | collective-permute-start | bytes 589832 | tf_op jit(solution)/shard_map/ppermute | solution.py:263
  44.2 0.6 copy-start.13
  44.2 4.8 %collective-permute-start.6 = (f32[128,8,128]{2,1,0:T(8,128)}, f32[128,8,128]{2,1,0:T(8,128)}, u32[]{:S(2)}, u32[]{:S(2)}) collective-permute-start(f32[128,8,128]{2,1,0:T(8,128)} %bitcast.8.own_ref), channel_id=1, source_target_pairs={{1,0},{0,1},{3,2},{2,3},{5,4},{4,5},{7,6},{6,7},{9,8},{8,9},{11,10... | collective-permute-start | bytes 1572872 | tf_op jit(solution)/shard_map/ppermute | solution.py:263
  44.9 21.8 %collective-permute-start.9 = (f32[768,512]{1,0:T(8,128)}, f32[768,512]{1,0:T(8,128)S(1)}, u32[]{:S(2)}, u32[]{:S(2)}) collective-permute-start(f32[768,512]{1,0:T(8,128)} %constant_dynamic-update-slice_fusion.refs_0_), channel_id=1, source_target_pairs={{24,0},{7,1},{26,2},{1,3},{28,4},{3,5},{30,6},{5,7},{0,8},{15,9},{... | collective-permute-start | bytes 4718600 | tf_op jit(solution)/shard_map/ppermute | solution.py:263
  46.0 20.6 %collective-permute-start.8 = (f32[768,512]{1,0:T(8,128)}, f32[768,512]{1,0:T(8,128)S(1)}, u32[]{:S(2)}, u32[]{:S(2)}) collective-permute-start(f32[768,512]{1,0:T(8,128)} %constant_dynamic-update-slice_fusion.refs_0_), channel_id=1, source_target_pairs={{8,0},{3,1},{10,2},{5,3},{12,4},{7,5},{14,6},{1,7},{16,8},{11,9},{... | collective-permute-start | bytes 4718600 | tf_op jit(solution)/shard_map/ppermute | solution.py:263
  47.6 8.7 %copy-start.14 = (f32[32,512]{1,0:T(8,128)S(1)}, f32[32,512]{1,0:T(8,128)}, u32[]{:S(2)}) copy-start(f32[32,512]{1,0:T(8,128)} %copy-done.13) | copy-start | bytes 196612
  47.6 39.6 %collective-permute-start.14 = (f32[768,512]{1,0:T(8,128)}, f32[768,512]{1,0:T(8,128)}, u32[]{:S(2)}, u32[]{:S(2)}) collective-permute-start(f32[768,512]{1,0:T(8,128)} %constant_dynamic-update-slice_fusion.refs_0_), channel_id=1, source_target_pairs={{1,0},{0,1},{3,2},{2,3},{5,4},{4,5},{7,6},{6,7},{9,8},{8,9},{11,10... | collective-permute-start | bytes 4718600 | tf_op jit(solution)/shard_map/ppermute | solution.py:263
  56.3 10.3 %collective-permute-start.7 = (f32[1,32,512]{2,1,0:T(8,128)S(1)}, f32[1,32,512]{2,1,0:T(8,128)S(1)}, u32[]{:S(2)}, u32[]{:S(2)}) collective-permute-start(f32[1,32,512]{2,1,0:T(8,128)S(1)} %bitcast.25), channel_id=1, source_target_pairs={{128,0},{129,1},{130,2},{131,3},{132,4},{133,5},{134,6},{135,7},{1... | collective-permute-start | bytes 196616 | tf_op jit(solution)/shard_map/ppermute | solution.py:263
  66.6 5.6 %copy-start.1 = (f32[512,512]{1,0:T(8,128)}, f32[512,512]{1,0:T(8,128)S(1)}, u32[]{:S(2)}) copy-start(f32[512,512]{1,0:T(8,128)S(1)} %get-tuple-element.56.i_in) | copy-start | bytes 3145732
  66.6 5.6 %copy-start.5 = (f32[512,512]{1,0:T(8,128)}, f32[512,512]{1,0:T(8,128)S(1)}, u32[]{:S(2)}) copy-start(f32[512,512]{1,0:T(8,128)S(1)} %get-tuple-element.55.l_in) | copy-start | bytes 3145732
  66.6 5.6 %copy-start.7 = (f32[512,512]{1,0:T(8,128)}, f32[512,512]{1,0:T(8,128)S(1)}, u32[]{:S(2)}) copy-start(f32[512,512]{1,0:T(8,128)S(1)} %get-tuple-element.54.w_in) | copy-start | bytes 3145732
  66.6 5.6 %copy-start.9 = (f32[2,32,512]{2,1,0:T(8,128)}, f32[2,32,512]{2,1,0:T(8,128)S(1)}, u32[]{:S(2)}) copy-start(f32[2,32,512]{2,1,0:T(8,128)S(1)} %pad_maximum_fusion.1) | copy-start | bytes 393220
  66.7 10.0 %collective-permute-start.10 = (f32[2,32,512]{2,1,0:T(8,128)S(1)}, f32[2,32,512]{2,1,0:T(8,128)S(1)}, u32[]{:S(2)}, u32[]{:S(2)}) collective-permute-start(f32[2,32,512]{2,1,0:T(8,128)S(1)} %pad_maximum_fusion.1), channel_id=1, source_target_pairs={{64,0},{65,1},{66,2},{67,3},{68,4},{69,5},{70,6},{71,7},{72,8},{73... | collective-permute-start | bytes 393224 | tf_op jit(solution)/shard_map/ppermute | solution.py:263
  71.3 15.1 %collective-permute-start.12 = (f32[384,512]{1,0:T(8,128)}, f32[384,512]{1,0:T(8,128)}, u32[]{:S(2)}, u32[]{:S(2)}) collective-permute-start(f32[384,512]{1,0:T(8,128)} %slice.48), channel_id=1, source_target_pairs={{24,0},{7,1},{26,2},{1,3},{28,4},{3,5},{30,6},{5,7},{0,8},{15,9},{... | collective-permute-start | bytes 2359304 | tf_op jit(solution)/shard_map/ppermute | solution.py:263
  72.2 14.8 %collective-permute-start.13 = (f32[384,512]{1,0:T(8,128)}, f32[384,512]{1,0:T(8,128)}, u32[]{:S(2)}, u32[]{:S(2)}) collective-permute-start(f32[384,512]{1,0:T(8,128)} %slice.49), channel_id=1, source_target_pairs={{8,0},{3,1},{10,2},{5,3},{12,4},{7,5},{14,6},{1,7},{16,8},{11,9},{... | collective-permute-start | bytes 2359304 | tf_op jit(solution)/shard_map/ppermute | solution.py:263
  75.0 21.1 %collective-permute-start.15 = (f32[768,512]{1,0:T(8,128)S(1)}, f32[768,512]{1,0:T(8,128)}, u32[]{:S(2)}, u32[]{:S(2)}) collective-permute-start(f32[768,512]{1,0:T(8,128)S(1)} %collective-permute-done.8.refs_1_), channel_id=1, source_target_pairs={{1,0},{0,1},{3,2},{2,3},{5,4},{4,5},{7,6},{6,7},{9,8},{8,9},{11,10... | collective-permute-start | bytes 4718600 | tf_op jit(solution)/shard_map/ppermute | solution.py:263
  76.6 0.7 copy-start.11
  77.3 18.7 %collective-permute-start.18 = (f32[768,512]{1,0:T(8,128)S(1)}, f32[768,512]{1,0:T(8,128)}, u32[]{:S(2)}, u32[]{:S(2)}) collective-permute-start(f32[768,512]{1,0:T(8,128)S(1)} %collective-permute-done.9.refs_4_), channel_id=1, source_target_pairs={{1,0},{0,1},{3,2},{2,3},{5,4},{4,5},{7,6},{6,7},{9,8},{8,9},{11,10... | collective-permute-start | bytes 4718600 | tf_op jit(solution)/shard_map/ppermute | solution.py:263
  77.3 1.2 %copy-start.2 = (f32[512,512]{1,0:T(8,128)S(1)}, f32[512,512]{1,0:T(8,128)}, u32[]{:S(2)}) copy-start(f32[512,512]{1,0:T(8,128)} %copy-done.1) | copy-start | bytes 3145732
  78.5 1.2 %copy-start.6 = (f32[512,512]{1,0:T(8,128)S(1)}, f32[512,512]{1,0:T(8,128)}, u32[]{:S(2)}) copy-start(f32[512,512]{1,0:T(8,128)} %copy-done.5) | copy-start | bytes 3145732
  79.8 1.2 %copy-start.8 = (f32[512,512]{1,0:T(8,128)S(1)}, f32[512,512]{1,0:T(8,128)}, u32[]{:S(2)}) copy-start(f32[512,512]{1,0:T(8,128)} %copy-done.7) | copy-start | bytes 3145732
  81.0 6.1 %copy-start.10 = (f32[2,32,512]{2,1,0:T(8,128)S(1)}, f32[2,32,512]{2,1,0:T(8,128)}, u32[]{:S(2)}) copy-start(f32[2,32,512]{2,1,0:T(8,128)} %copy-done.9) | copy-start | bytes 393220
  81.0 6.1 %copy-start.12 = (f32[2,32,512]{2,1,0:T(8,128)S(1)}, f32[2,32,512]{2,1,0:T(8,128)}, u32[]{:S(2)}) copy-start(f32[2,32,512]{2,1,0:T(8,128)} %copy-done.11) | copy-start | bytes 393220
  86.4 9.6 %collective-permute-start.16 = (f32[384,512]{1,0:T(8,128)}, f32[384,512]{1,0:T(8,128)S(1)}, u32[]{:S(2)}, u32[]{:S(2)}) collective-permute-start(f32[384,512]{1,0:T(8,128)} %collective-permute-done.12.refs_2_), channel_id=1, source_target_pairs={{1,0},{0,1},{3,2},{2,3},{5,4},{4,5},{7,6},{6,7},{9,8},{8,9},{11,10... | collective-permute-start | bytes 2359304 | tf_op jit(solution)/shard_map/ppermute | solution.py:263
  87.0 9.0 %collective-permute-start.17 = (f32[384,512]{1,0:T(8,128)}, f32[384,512]{1,0:T(8,128)S(1)}, u32[]{:S(2)}, u32[]{:S(2)}) collective-permute-start(f32[384,512]{1,0:T(8,128)} %collective-permute-done.13.refs_3_), channel_id=1, source_target_pairs={{1,0},{0,1},{3,2},{2,3},{5,4},{4,5},{7,6},{6,7},{9,8},{8,9},{11,10... | collective-permute-start | bytes 2359304 | tf_op jit(solution)/shard_map/ppermute | solution.py:263
  87.1 8.9 %slice-start = ((s8[6291456]{0:T(1024)(128)(4,1)}), s8[4194304]{0:T(1024)(128)(4,1)S(1)}, s32[]{:S(2)}) async-start(s8[6291456]{0:T(1024)(128)(4,1)} %bitcast.17), calls=%async_computation.2 | async-start | bytes 8388608
  87.2 8.9 %slice-start.1 = ((s8[6291456]{0:T(1024)(128)(4,1)}), s8[2097152]{0:T(1024)(128)(4,1)S(1)}, s32[]{:S(2)}) async-start(s8[6291456]{0:T(1024)(128)(4,1)} %bitcast.17), calls=%async_computation.3 | async-start | bytes 4194304
  87.2 8.8 %collective-permute-start.11 = (f32[4,32,512]{2,1,0:T(8,128)S(1)}, f32[4,32,512]{2,1,0:T(8,128)S(1)}, u32[]{:S(2)}, u32[]{:S(2)}) collective-permute-start(f32[4,32,512]{2,1,0:T(8,128)S(1)} %pad_maximum_fusion.near), channel_id=1, source_target_pairs={{32,0},{33,1},{34,2},{35,3},{36,4},{37,5},{38,6},{39,7},{40,8},{41... | collective-permute-start | bytes 786440 | tf_op jit(solution)/shard_map/ppermute | solution.py:263
  94.4 1.0 copy-start.3
  96.1 1.2 %copy-start.4 = (f32[512,512]{1,0:T(8,128)S(1)}, f32[512,512]{1,0:T(8,128)}, u32[]{:S(2)}) copy-start(f32[512,512]{1,0:T(8,128)} %copy-done.3) | copy-start | bytes 3145732
